TPU v7x, 32 devices: a whole 2x2x4 slice. The times are simulated.
32 devices in a mesh: groups: 2 (over x), shard: 16 (over z, y, core).
Axes of the slice: x: 2, y: 2, z: 4, core: 2. Of those that a mesh axis runs over, the one named last changes fastest.
Arguments:
- tokens: bfloat16 [8192, 8192], P(('groups', 'shard')), parts along dimension 0, may hold values from -6 to 6
- cotangent: bfloat16 [8192, 1024], P(('groups', 'shard')), parts along dimension 0, may hold values from -6 to 6
- response_loss_mask: int32 [8192], P(('groups', 'shard')), parts along dimension 0, may hold values 0 or 1
- adapter_down_weight: bfloat16 [64, 8192], P(None, 'shard'), may hold values from -0.0625 to 0.0625
- projection: bfloat16 [65536, 4096], P('shard'), may hold values from -0.0234375 to 0.0234375
- targets: float32 [256, 4096], P(('groups', 'shard')), parts along dimension 0, may hold values from -6 to 6
Outputs:
- scores: float32 [32, 128], P('groups', 'shard'), parts along dimension 0
There are 2 independent parts, one for each index of `groups`. A program takes and returns all parts, laid end to end along the dimension named above; an argument that names none is the same for every part. Nothing has to cross between parts.
All inputs are finite; a program needn't handle non-finite values. No bound on the sum of `response_loss_mask` on one device may be relied on, other than what follows from the above.
Results may differ from a plain program's by a relative error of at most 0.004.
Values may be sent and summed in bfloat16 or wider, within the bound.
No kernel may reach another device: no remote copies, remote signals or barrier semaphores. Data moves between devices by JAX's collectives and lax.ppermute only.
A program may use at most 128 MiB of HBM per device.

v0:
```python
import functools

import jax
import jax.numpy as jnp
from jax import lax
from jax.experimental import pallas as pl
from jax.experimental.pallas import tpu as pltpu
from jax.sharding import PartitionSpec as P

PDIM = 4096
LENGTH = 256
LANES = 256
NEAR = 4
MIB = 1 << 20
HIDE = 30 * 10**9
NT = (((1,), (1,)), ((), ()))
VMEM = pl.BlockSpec(memory_space=pltpu.VMEM)
SMEM = pl.BlockSpec(memory_space=pltpu.SMEM)
ANY = pl.BlockSpec(memory_space=pl.ANY)


def swap(value, bit, n):
    return lax.ppermute(value, "shard", [(s, s ^ bit) for s in range(n)])


def span(bits):
    sums = [0]
    for bit in bits:
        sums += [k + bit for k in sums]
    return sums


def in_hbm(value):
    return pltpu.with_memory_space_constraint(value, pltpu.HBM)


def in_vmem(value):
    return pltpu.with_memory_space_constraint(value, pltpu.VMEM)


def load_kernel(count, starts, *refs):
    sources, outs, sems = refs[:count], refs[-1 - count : -1], refs[-1]
    copies = []
    for source, start, out in zip(sources, starts, outs):
        rows = out.shape[0]
        step = min(rows, LANES // 2)
        for i in range(0, rows, step):
            part = source.at[pl.ds(start + i, step)]
            copies.append(pltpu.make_async_copy(part, out.at[pl.ds(i, step)], sems.at[len(copies)]))
    for copy in copies:
        copy.start()
    for copy in copies:
        copy.wait()


def load(name, parts, after):
    size = sum(rows * array.size // array.shape[0] * array.dtype.itemsize for array, _, rows in parts)
    pieces = sum(max(rows // (LANES // 2), 1) for _, _, rows in parts)
    return pl.pallas_call(
        functools.partial(load_kernel, len(parts), [start for _, start, _ in parts]),
        out_shape=[pltpu.VMEM((rows,) + array.shape[1:], array.dtype) for array, _, rows in parts],
        in_specs=[ANY] * (len(parts) + len(after)),
        out_specs=[VMEM] * len(parts),
        scratch_shapes=[pltpu.SemaphoreType.DMA((pieces,))],
        compiler_params=pltpu.CompilerParams(vmem_limit_bytes=MIB),
        cost_estimate=pl.CostEstimate(flops=0, bytes_accessed=2 * size, transcendentals=0),
        name=name,
    )(*[in_hbm(array) for array, _, _ in parts], *after)


def hold(name, value, after, flops=0):
    return pl.pallas_call(
        lambda *refs: None,
        out_shape=jax.ShapeDtypeStruct(value.shape, value.dtype),
        in_specs=[ANY] * (1 + len(after)),
        out_specs=ANY,
        input_output_aliases={0: 0},
        compiler_params=pltpu.CompilerParams(vmem_limit_bytes=MIB),
        cost_estimate=pl.CostEstimate(flops=flops, bytes_accessed=2000000, transcendentals=0),
        name=name,
    )(value, *after)


def join_kernel(picks, *refs):
    for pick, out in zip(picks, refs[-len(picks) :]):
        for target, (source, *entry) in enumerate(pick):
            out[target] = refs[source][entry[0]] if entry else refs[source][...]


def join(name, values, picks, shape, after=(), flops=0):
    return pl.pallas_call(
        functools.partial(join_kernel, picks),
        out_shape=[jax.ShapeDtypeStruct((len(pick),) + shape, values[0].dtype) for pick in picks],
        in_specs=[VMEM] * len(values) + [ANY] * len(after),
        out_specs=[VMEM] * len(picks),
        compiler_params=pltpu.CompilerParams(vmem_limit_bytes=2 * MIB),
        cost_estimate=pl.CostEstimate(flops=flops, bytes_accessed=2000000, transcendentals=0),
        name=name,
    )(*values, *after)


def add_lowrank(total, me, blocks, places, tokens):
    for block, owners in zip(blocks, places):
        depth = block.shape[-1]
        for i, k in enumerate(owners):
            start = pl.multiple_of((me[0] ^ k) * depth, depth)
            part = block[i] if len(block.shape) == 3 else block[...]
            total += lax.dot_general(part, tokens[:, pl.ds(start, depth)], NT, preferred_element_type=jnp.float32)
    return total


def lowrank_kernel(places, me, tokens, *refs):
    blocks, out = refs[: len(places)], refs[-1]
    before = refs[len(places)][...] if len(refs) > len(places) + 1 else jnp.zeros(out.shape, jnp.float32)
    out[...] = add_lowrank(before, me, blocks, places, tokens)


def partial_lowrank(name, me, tokens, blocks, places, before=()):
    return pl.pallas_call(
        functools.partial(lowrank_kernel, places),
        out_shape=jax.ShapeDtypeStruct((blocks[0].shape[-2], tokens.shape[0]), jnp.float32),
        in_specs=[SMEM] + [VMEM] * (1 + len(blocks) + len(before)),
        out_specs=VMEM,
        compiler_params=pltpu.CompilerParams(vmem_limit_bytes=2 * MIB),
        cost_estimate=pl.CostEstimate(flops=100000000, bytes_accessed=2000000, transcendentals=0),
        name=name,
    )(me, tokens, *blocks, *before)


def grads_kernel(owners, places, me, tokens, *refs):
    blocks = refs[: len(places)]
    before, cotangent, mask = refs[len(places) : len(places) + 3]
    outs, grads = refs[-1 - len(owners) : -1], refs[-1]
    total = add_lowrank(before[...], me, blocks, places, tokens)
    rank = total.shape[0]
    lowrank = total.astype(jnp.bfloat16) * mask[...].astype(jnp.bfloat16)
    turned = jnp.dot(lowrank, cotangent[...], preferred_element_type=jnp.float32)
    grads[...] = turned.T
    pack = LANES // rank
    share = outs[0].shape[1]
    for out, ks in zip(outs, owners):
        for i, k in enumerate(ks):
            start = pl.multiple_of((me[0] ^ k) * (share * pack), share * pack)
            for q in range(pack):
                rows = grads[pl.ds(start + q, share, stride=pack), :]
                out[i, :, q * rank : (q + 1) * rank] = rows.astype(jnp.bfloat16)


def packed_grads(me, owners, tokens, blocks, places, before, cotangent, mask):
    rank, width = blocks[0].shape[-2], cotangent.shape[1]
    share = width * rank // LANES // sum(len(ks) for ks in owners)
    return pl.pallas_call(
        functools.partial(grads_kernel, owners, places),
        out_shape=[jax.ShapeDtypeStruct((len(ks), share, LANES), jnp.bfloat16) for ks in owners],
        in_specs=[SMEM] + [VMEM] * (len(blocks) + 4),
        out_specs=[VMEM] * len(owners),
        scratch_shapes=[pltpu.VMEM((width, rank), jnp.float32)],
        compiler_params=pltpu.CompilerParams(vmem_limit_bytes=6 * MIB),
        cost_estimate=pl.CostEstimate(flops=100000000, bytes_accessed=2000000, transcendentals=0),
        name="grads",
    )(me, tokens, *blocks, before, cotangent, mask)


def features_kernel(places, count, me, *refs):
    arrays, weights = refs[:count], refs[count]
    keep, send, x, left, total = refs[-5:]
    n = len(places)
    share = arrays[0].shape[1]
    pitch = x.shape[1] // n
    for k, (source, entry) in enumerate(places):
        rows = arrays[source][entry]
        place = pl.multiple_of((me[0] ^ k) * pitch, pitch)
        for h in range(x.shape[0]):
            x[h, pl.ds(place, share), :] = rows[:, h * 128 : (h + 1) * 128].astype(jnp.float32)
    for j in range(share):
        for h in range(x.shape[0]):
            at = j * LANES + h * 128
            left[:, at : at + 128] = x[h, pl.ds(j, n, stride=pitch), :].astype(jnp.bfloat16)
    total[...] = jnp.dot(left[...], weights[...], preferred_element_type=jnp.float32)
    part = keep.shape[1]
    mine = pl.multiple_of((me[0] & 1) * part, part)
    partner = pl.multiple_of((1 - (me[0] & 1)) * part, part)
    keep[...] = total[:, pl.ds(mine, part)]
    send[...] = total[:, pl.ds(partner, part)].astype(jnp.bfloat16)


def partial_features(me, arrays, places, projection, after):
    n = len(places)
    share = arrays[0].shape[1]
    depth, width = projection.shape
    half = (n, width // 2)
    return pl.pallas_call(
        functools.partial(features_kernel, places, len(arrays)),
        out_shape=[jax.ShapeDtypeStruct(half, jnp.float32), jax.ShapeDtypeStruct(half, jnp.bfloat16)],
        in_specs=[SMEM] + [VMEM] * (len(arrays) + 1) + [ANY],
        out_specs=[VMEM, VMEM],
        scratch_shapes=[
            pltpu.VMEM((LANES // 128, n * max(share, 8), 128), jnp.float32),
            pltpu.VMEM((n, depth), jnp.bfloat16),
            pltpu.VMEM((n, width), jnp.float32),
        ],
        compiler_params=pltpu.CompilerParams(vmem_limit_bytes=4 * MIB),
        cost_estimate=pl.CostEstimate(flops=600000000, bytes_accessed=34000000, transcendentals=0),
        name="features",
    )(me, *arrays, in_vmem(projection), after)


def scores_kernel(me, targets, partner_targets, kept, *refs):
    mine, send = refs[-2:]
    features = kept[...]
    for arrived in refs[:-2]:
        features += arrived[...].astype(jnp.float32)
    count, half = features.shape
    start = pl.multiple_of((me[0] & 1) * half, half)
    high = lax.Precision.HIGHEST
    ones = jnp.ones((targets.shape[0], half), jnp.float32)
    squares = lax.dot_general(ones, features * features, NT, precision=high, preferred_element_type=jnp.float32)
    rest = jnp.zeros((targets.shape[0], mine.shape[1] - 2 * count), jnp.float32)
    for source, out in ((targets, mine), (partner_targets, send)):
        scale = lax.rsqrt(jnp.sum(source[...] * source[...], axis=1, keepdims=True) / PDIM + 1e-06)
        dots = lax.dot_general(
            source[:, pl.ds(start, half)], features, NT, precision=high, preferred_element_type=jnp.float32
        )
        parts = [dots * scale, squares] + ([rest] if rest.shape[1] else [])
        out[...] = jnp.concatenate(parts, axis=1)


def partial_scores(me, targets, partner_targets, kept, arrived):
    shape = jax.ShapeDtypeStruct((targets.shape[0], 128), jnp.float32)
    return pl.pallas_call(
        scores_kernel,
        out_shape=[shape, shape],
        in_specs=[SMEM] + [VMEM] * (3 + len(arrived)),
        out_specs=[VMEM, VMEM],
        compiler_params=pltpu.CompilerParams(vmem_limit_bytes=6 * MIB),
        name="partial_scores",
    )(me, targets, partner_targets, kept, *arrived)


def body(tokens, cotangent, response_loss_mask, adapter_down_weight, projection, targets):
    n = lax.axis_size("shard")
    far = n // NEAR
    me = lax.axis_index("shard").astype(jnp.int32).reshape(1)
    block = adapter_down_weight
    bits = [1 << i for i in range(n.bit_length() - 1)]

    whole = [(tokens, 0, tokens.shape[0]), (cotangent, 0, cotangent.shape[0])]
    whole += [(response_loss_mask.reshape(1, -1), 0, 1), (targets, 0, targets.shape[0])]
    tokens, cotangent, mask, targets = load("load_1", whole, (me,))
    order = [far - 1] + list(range(1, far - 1)) + [0]
    column = [swap(block, NEAR * d, n) for d in order[:-1]] + [block]
    across = [swap(value, 2, n) for value in column]
    places = [[[NEAR * d + k] for d in order] for k in range(NEAR)]
    blocks, owners = column + across[:1] + across[-1:], places[0] + places[2][:1] + places[2][-1:]
    total = partial_lowrank("lowrank_1", me, tokens, blocks, owners)
    picks = [[(i,) for i in range(far)]]
    (line,) = join("join_column", column, picks, block.shape, (total,))
    (gathered,) = join("join_across", across, picks, block.shape)
    other = [swap(line, 1, n), swap(gathered, 1, n)]
    total = partial_lowrank("lowrank_2", me, tokens, across[1:-1], places[2][1:-1], (total,))
    owners = [[k + 1 for part in side for k in part] for side in (places[0], places[2])]
    total = partial_lowrank("lowrank_3", me, tokens, other[:1], owners[:1], (total,))

    stages = [bits[i : i + 2] for i in range(2, len(bits), 2)] + [bits[:2]]
    left = span([b for stage in stages[1:] for b in stage])
    moves = span(stages[0])
    targets_of = [[m ^ r for r in left] for m in moves]
    rows = packed_grads(me, targets_of, tokens, other[1:], owners[1:], total, cotangent, mask)
    rows = list(rows)
    rows[-1] = hold("hold_rows", rows[-1], (), HIDE)
    arrays = [swap(array, m, n) for array, m in zip(rows[:0:-1], moves[:0:-1])] + [rows[0]]
    held = {(m, r): (a, i) for a, m in enumerate(moves[::-1]) for i, r in enumerate(left)}
    for number, stage in enumerate(stages[1:]):
        moves, left = span(stage), span([b for later in stages[number + 2 :] for b in later])
        pairs = [[(src, r ^ m) for src in sorted({s for s, _ in held}) for r in left] for m in moves]
        picks = [[held[pair] for pair in group] for group in pairs[1:]]
        sent = join(f"join_rows_{number}", arrays, picks, rows[0].shape[1:])
        came = [swap(array, m, n) for array, m in zip(sent[::-1], moves[:0:-1])]
        kept = {pair: (held[pair][0] + len(came), held[pair][1]) for pair in pairs[0]}
        for a, (m, group) in enumerate(zip(moves[:0:-1], pairs[:0:-1])):
            kept.update({(src ^ m, r ^ m): (a, i) for i, (src, r) in enumerate(group)})
        arrays, held = came + arrays, kept
    partner_targets = swap(targets, 1, n)

    places = [held[k, 0] for k in range(n)]
    kept, send = partial_features(me, arrays, places, projection, partner_targets)
    kept = kept + swap(send, 1, n).astype(jnp.float32)
    for stage in [bits[1:3]] + [[bit] for bit in bits[3:]]:
        half = kept.astype(jnp.bfloat16)
        arrived = [swap(half, m, n) for m in span(stage)[:0:-1]]
        if bits[-1] not in stage:
            for value in arrived:
                kept = kept + value.astype(jnp.float32)
    mine, send = partial_scores(me, targets, partner_targets, kept, arrived)
    total = mine + swap(send, 1, n)
    scale = lax.rsqrt(total[:, n : 2 * n] / PDIM + 1e-06)
    return (total[:, :n] * scale / PDIM).T


def solution(mesh):
    in_specs = (
        P(("groups", "shard"), None),
        P(("groups", "shard"), None),
        P(("groups", "shard")),
        P(None, "shard"),
        P("shard", None),
        P(("groups", "shard"), None),
    )
    out_specs = P("groups", "shard")
    return jax.shard_map(body, mesh=mesh, in_specs=in_specs, out_specs=out_specs, check_vma=False)
```

profile of v0, /device:TPU:0, one launch (start us, length us, event | category | flops | bytes accessed | tf_op | source)
XLA Modules:
  0.0 51.7 jit_solution(15049312123968402878)
XLA Ops:
  0.0 5.0 %collective-permute-start.1 = (bf16[64,512]{1,0:T(8,128)(2,1)}, bf16[64,512]{1,0:T(8,128)(2,1)S(1)}, u32[]{:S(2)}, u32[]{:S(2)}) collective-permute-start(bf16[64,512]{1,0:T(8,128)(2,1)} %refs_3_.5), channel_id=1, source_target_pairs={{0,12},{1,13},{2,14},{3,15},{4,8},{5,9},{6,10},{7,11},{8,4},{9,5},... | collective-permute-start | bytes 196616 | tf_op jit(solution)/shard_map/ppermute | solution.py:23
  5.7 1.7 %collective-permute-start.7 = (bf16[64,512]{1,0:T(8,128)(2,1)}, bf16[64,512]{1,0:T(8,128)(2,1)S(1)}, u32[]{:S(2)}, u32[]{:S(2)}) collective-permute-start(bf16[64,512]{1,0:T(8,128)(2,1)} %refs_3_.5), channel_id=1, source_target_pairs={{0,2},{1,3},{2,0},{3,1},{4,6},{5,7},{6,4},{7,5},{8,10},{9,11},{10,... | collective-permute-start | bytes 196616 | tf_op jit(solution)/shard_map/ppermute | solution.py:23
  7.4 0.9 %collective-permute-done.1.refs_0_ = bf16[64,512]{1,0:T(8,128)(2,1)S(1)} collective-permute-done((bf16[64,512]{1,0:T(8,128)(2,1)}, bf16[64,512]{1,0:T(8,128)(2,1)S(1)}, u32[]{:S(2)}, u32[]{:S(2)}) %collective-permute-start.1) | collective-permute-done | bytes 65568 | tf_op jit(solution)/shard_map/ppermute | solution.py:23
  8.2 1.5 %collective-permute-start.2 = (bf16[64,512]{1,0:T(8,128)(2,1)S(1)}, bf16[64,512]{1,0:T(8,128)(2,1)S(1)}, u32[]{:S(2)}, u32[]{:S(2)}) collective-permute-start(bf16[64,512]{1,0:T(8,128)(2,1)S(1)} %collective-permute-done.1.refs_0_), channel_id=1, source_target_pairs={{0,2},{1,3},{2,0},{3,1},{4,6},{5,7},{6,4},{7,5},{8,10},{9,11},{10,... | collective-permute-start | bytes 196616 | tf_op jit(solution)/shard_map/ppermute | solution.py:23
  10.0 1.6 %collective-permute-start.4 = (bf16[64,512]{1,0:T(8,128)(2,1)S(1)}, bf16[64,512]{1,0:T(8,128)(2,1)S(1)}, u32[]{:S(2)}, u32[]{:S(2)}) collective-permute-start(bf16[64,512]{1,0:T(8,128)(2,1)S(1)} %collective-permute-done.3.refs_1_), channel_id=1, source_target_pairs={{0,2},{1,3},{2,0},{3,1},{4,6},{5,7},{6,4},{7,5},{8,10},{9,11},{10,... | collective-permute-start | bytes 196616 | tf_op jit(solution)/shard_map/ppermute | solution.py:23
  11.6 0.8 %collective-permute-start.6 = (bf16[64,512]{1,0:T(8,128)(2,1)S(1)}, bf16[64,512]{1,0:T(8,128)(2,1)S(1)}, u32[]{:S(2)}, u32[]{:S(2)}) collective-permute-start(bf16[64,512]{1,0:T(8,128)(2,1)S(1)} %collective-permute-done.5.refs_2_), channel_id=1, source_target_pairs={{0,2},{1,3},{2,0},{3,1},{4,6},{5,7},{6,4},{7,5},{8,10},{9,11},{10,... | collective-permute-start | bytes 196616 | tf_op jit(solution)/shard_map/ppermute | solution.py:23
  12.4 2.4 %load_1.1 = (bf16[256,8192]{1,0:T(8,128)(2,1)S(1)}, bf16[256,1024]{1,0:T(8,128)(2,1)S(1)}, s32[1,256]{1,0:T(1,128)S(1)}, f32[8,4096]{1,0:T(8,128)S(1)}) custom-call(bf16[256,8192]{1,0:T(8,128)(2,1)} %refs_0_.1, bf16[256,1024]{1,0:T(8,128)(2,1)} %refs_1_.1, s32[1,256]{1,0:T(1,128)} %bitcast.6, f32[8,4096]{1,0:T(8,128)} %refs_3_.3, s32[1]{0:T(128)} %bitcast.refs_4_.me), custom_call_target="tpu_custom_call" | custom-call | bytes 9701376 | tf_op jit(solution)/shard_map/load_1/pallas_call | solution.py:59
  17.5 1.0 %grads.1 = (bf16[4,16,256]{2,1,0:T(8,128)(2,1)S(1)}, bf16[4,16,256]{2,1,0:T(8,128)(2,1)S(1)}, bf16[4,16,256]{2,1,0:T(8,128)(2,1)S(1)}, bf16[4,16,256]{2,1,0:T(8,128)(2,1)S(1)}) custom-call(s32[1]{0:T(128)} %bitcast.refs_4_.me, bf16[256,8192]{1,0:T(8,128)(2,1)S(1)} %get-tuple-element.21.tokens, bf16[4,64,512]{2,1,0:T(8,128)(2,1)S(1)} %collective-permute-done.8.refs_0_, ...), custom_call_target="tpu_custom_call" | custom-call | flops 100000000 | bytes 2000000 | tf_op jit(solution)/shard_map/grads/pallas_call | solution.py:152
  18.6 3.2 %collective-permute-start.10 = (bf16[4,16,256]{2,1,0:T(8,128)(2,1)S(1)}, bf16[4,16,256]{2,1,0:T(8,128)(2,1)S(1)}, u32[]{:S(2)}, u32[]{:S(2)}) collective-permute-start(bf16[4,16,256]{2,1,0:T(8,128)(2,1)S(1)} %hold_rows.1), channel_id=1, source_target_pairs={{0,12},{1,13},{2,14},{3,15},{4,8},{5,9},{6,10},{7,11},{8,4},{9,5},... | collective-permute-start | bytes 98312 | tf_op jit(solution)/shard_map/ppermute | solution.py:23
  21.9 1.2 %collective-permute-start.12 = (bf16[4,16,256]{2,1,0:T(8,128)(2,1)S(1)}, bf16[4,16,256]{2,1,0:T(8,128)(2,1)S(1)}, u32[]{:S(2)}, u32[]{:S(2)}) collective-permute-start(bf16[4,16,256]{2,1,0:T(8,128)(2,1)S(1)} %get-tuple-element.26), channel_id=1, source_target_pairs={{0,4},{1,5},{2,6},{3,7},{4,0},{5,1},{6,2},{7,3},{8,12},{9,13},{10,... | collective-permute-start | bytes 98312 | tf_op jit(solution)/shard_map/ppermute | solution.py:23
  23.1 1.7 %collective-permute-done.10.refs_0_.refs_3_ = bf16[4,16,256]{2,1,0:T(8,128)(2,1)S(1)} collective-permute-done((bf16[4,16,256]{2,1,0:T(8,128)(2,1)S(1)}, bf16[4,16,256]{2,1,0:T(8,128)(2,1)S(1)}, u32[]{:S(2)}, u32[]{:S(2)}) %collective-permute-start.10) | collective-permute-done | bytes 32800 | tf_op jit(solution)/shard_map/ppermute | solution.py:23
  24.8 1.9 %collective-permute-done.11.refs_1_.refs_4_ = bf16[4,16,256]{2,1,0:T(8,128)(2,1)S(1)} collective-permute-done((bf16[4,16,256]{2,1,0:T(8,128)(2,1)S(1)}, bf16[4,16,256]{2,1,0:T(8,128)(2,1)S(1)}, u32[]{:S(2)}, u32[]{:S(2)}) %collective-permute-start.11) | collective-permute-done | bytes 32800 | tf_op jit(solution)/shard_map/ppermute | solution.py:23
  27.6 1.0 %collective-permute-start.15 = (bf16[4,16,256]{2,1,0:T(8,128)(2,1)S(1)}, bf16[4,16,256]{2,1,0:T(8,128)(2,1)S(1)}, u32[]{:S(2)}, u32[]{:S(2)}) collective-permute-start(bf16[4,16,256]{2,1,0:T(8,128)(2,1)S(1)} %get-tuple-element.30), channel_id=1, source_target_pairs={{0,1},{1,0},{2,3},{3,2},{4,5},{5,4},{6,7},{7,6},{8,9},{9,8},{10,11... | collective-permute-start | bytes 98312 | tf_op jit(solution)/shard_map/ppermute | solution.py:23
  28.6 1.5 %collective-permute-done.13.refs_0_ = bf16[4,16,256]{2,1,0:T(8,128)(2,1)S(1)} collective-permute-done((bf16[4,16,256]{2,1,0:T(8,128)(2,1)S(1)}, bf16[4,16,256]{2,1,0:T(8,128)(2,1)S(1)}, u32[]{:S(2)}, u32[]{:S(2)}) %collective-permute-start.13) | collective-permute-done | bytes 32800 | tf_op jit(solution)/shard_map/ppermute | solution.py:23
  30.1 0.8 %collective-permute-done.14.refs_1_ = bf16[4,16,256]{2,1,0:T(8,128)(2,1)S(1)} collective-permute-done((bf16[4,16,256]{2,1,0:T(8,128)(2,1)S(1)}, bf16[4,16,256]{2,1,0:T(8,128)(2,1)S(1)}, u32[]{:S(2)}, u32[]{:S(2)}) %collective-permute-start.14) | collective-permute-done | bytes 32800 | tf_op jit(solution)/shard_map/ppermute | solution.py:23
  31.0 4.5 %features.1 = (f32[16,2048]{1,0:T(8,128)S(1)}, bf16[16,2048]{1,0:T(8,128)(2,1)S(1)}) custom-call(s32[1]{0:T(128)} %bitcast.refs_4_.me, bf16[4,16,256]{2,1,0:T(8,128)(2,1)S(1)} %collective-permute-done.13.refs_0_, bf16[4,16,256]{2,1,0:T(8,128)(2,1)S(1)} %collective-permute-done.14.refs_1_, bf16[4,16,256]{2,1,0:T(8,128)(2,1)S(1)} %collective-permute-done.15.refs_2_, ...), custom_call_target="tpu_custom_call" | custom-call | flops 600000000 | bytes 34000000 | tf_op jit(solution)/shard_map/features/pallas_call | solution.py:192
  35.5 1.2 %collective-permute-done.16 = bf16[16,2048]{1,0:T(8,128)(2,1)S(1)} collective-permute-done((bf16[16,2048]{1,0:T(8,128)(2,1)S(1)}, bf16[16,2048]{1,0:T(8,128)(2,1)S(1)}, u32[]{:S(2)}, u32[]{:S(2)}) %collective-permute-start.16) | collective-permute-done | bytes 65568 | tf_op jit(solution)/shard_map/ppermute | solution.py:23
  36.8 1.1 %collective-permute-start.17 = (bf16[16,2048]{1,0:T(8,128)(2,1)S(1)}, bf16[16,2048]{1,0:T(8,128)(2,1)S(1)}, u32[]{:S(2)}, u32[]{:S(2)}) collective-permute-start(bf16[16,2048]{1,0:T(8,128)(2,1)S(1)} %fusion), channel_id=1, source_target_pairs={{0,6},{1,7},{2,4},{3,5},{4,2},{5,3},{6,0},{7,1},{8,14},{9,15},{10,... | collective-permute-start | bytes 196616 | tf_op jit(solution)/shard_map/ppermute | solution.py:23
  37.9 1.1 %collective-permute-start.18 = (bf16[16,2048]{1,0:T(8,128)(2,1)S(1)}, bf16[16,2048]{1,0:T(8,128)(2,1)S(1)}, u32[]{:S(2)}, u32[]{:S(2)}) collective-permute-start(bf16[16,2048]{1,0:T(8,128)(2,1)S(1)} %fusion), channel_id=1, source_target_pairs={{0,4},{1,5},{2,6},{3,7},{4,0},{5,1},{6,2},{7,3},{8,12},{9,13},{10,... | collective-permute-start | bytes 196616 | tf_op jit(solution)/shard_map/ppermute | solution.py:23
  38.9 1.4 %collective-permute-start.19 = (bf16[16,2048]{1,0:T(8,128)(2,1)S(1)}, bf16[16,2048]{1,0:T(8,128)(2,1)S(1)}, u32[]{:S(2)}, u32[]{:S(2)}) collective-permute-start(bf16[16,2048]{1,0:T(8,128)(2,1)S(1)} %fusion), channel_id=1, source_target_pairs={{0,2},{1,3},{2,0},{3,1},{4,6},{5,7},{6,4},{7,5},{8,10},{9,11},{10,... | collective-permute-start | bytes 196616 | tf_op jit(solution)/shard_map/ppermute | solution.py:23
  40.4 2.3 %collective-permute-done.17 = bf16[16,2048]{1,0:T(8,128)(2,1)S(1)} collective-permute-done((bf16[16,2048]{1,0:T(8,128)(2,1)S(1)}, bf16[16,2048]{1,0:T(8,128)(2,1)S(1)}, u32[]{:S(2)}, u32[]{:S(2)}) %collective-permute-start.17) | collective-permute-done | bytes 65568 | tf_op jit(solution)/shard_map/ppermute | solution.py:23
  43.4 2.1 %collective-permute-start.20 = (bf16[16,2048]{1,0:T(8,128)(2,1)S(1)}, bf16[16,2048]{1,0:T(8,128)(2,1)S(1)}, u32[]{:S(2)}, u32[]{:S(2)}) collective-permute-start(bf16[16,2048]{1,0:T(8,128)(2,1)S(1)} %get-tuple-element.35), channel_id=1, source_target_pairs={{0,8},{1,9},{2,10},{3,11},{4,12},{5,13},{6,14},{7,15},{8,0},{9,1},... | collective-permute-start | bytes 196616 | tf_op jit(solution)/shard_map/ppermute | solution.py:23
  45.5 3.8 %collective-permute-done.20.refs_0_ = bf16[16,2048]{1,0:T(8,128)(2,1)S(1)} collective-permute-done((bf16[16,2048]{1,0:T(8,128)(2,1)S(1)}, bf16[16,2048]{1,0:T(8,128)(2,1)S(1)}, u32[]{:S(2)}, u32[]{:S(2)}) %collective-permute-start.20) | collective-permute-done | bytes 65568 | tf_op jit(solution)/shard_map/ppermute | solution.py:23
  49.9 1.2 %collective-permute-done.21 = f32[8,128]{1,0:T(8,128)S(1)} collective-permute-done((f32[8,128]{1,0:T(8,128)S(1)}, f32[8,128]{1,0:T(8,128)S(1)}, u32[]{:S(2)}, u32[]{:S(2)}) %collective-permute-start.21) | collective-permute-done | bytes 4128 | tf_op jit(solution)/shard_map/ppermute | solution.py:23
  (54 shorter events, 6.5 us)
Async XLA Ops:
  0.0 14.8 %copy-start = (bf16[64,512]{1,0:T(8,128)(2,1)S(1)}, bf16[64,512]{1,0:T(8,128)(2,1)}, u32[]{:S(2)}) copy-start(bf16[64,512]{1,0:T(8,128)(2,1)} %refs_3_.5) | copy-start | bytes 196612
  0.0 8.2 %collective-permute-start.1 = (bf16[64,512]{1,0:T(8,128)(2,1)}, bf16[64,512]{1,0:T(8,128)(2,1)S(1)}, u32[]{:S(2)}, u32[]{:S(2)}) collective-permute-start(bf16[64,512]{1,0:T(8,128)(2,1)} %refs_3_.5), channel_id=1, source_target_pairs={{0,12},{1,13},{2,14},{3,15},{4,8},{5,9},{6,10},{7,11},{8,4},{9,5},... | collective-permute-start | bytes 196616 | tf_op jit(solution)/shard_map/ppermute | solution.py:23
  5.1 4.9 %collective-permute-start.3 = (bf16[64,512]{1,0:T(8,128)(2,1)}, bf16[64,512]{1,0:T(8,128)(2,1)S(1)}, u32[]{:S(2)}, u32[]{:S(2)}) collective-permute-start(bf16[64,512]{1,0:T(8,128)(2,1)} %refs_3_.5), channel_id=1, source_target_pairs={{0,4},{1,5},{2,6},{3,7},{4,0},{5,1},{6,2},{7,3},{8,12},{9,13},{10,... | collective-permute-start | bytes 196616 | tf_op jit(solution)/shard_map/ppermute | solution.py:23
  5.1 6.5 %collective-permute-start.5 = (bf16[64,512]{1,0:T(8,128)(2,1)}, bf16[64,512]{1,0:T(8,128)(2,1)S(1)}, u32[]{:S(2)}, u32[]{:S(2)}) collective-permute-start(bf16[64,512]{1,0:T(8,128)(2,1)} %refs_3_.5), channel_id=1, source_target_pairs={{0,8},{1,9},{2,10},{3,11},{4,12},{5,13},{6,14},{7,15},{8,0},{9,1},... | collective-permute-start | bytes 196616 | tf_op jit(solution)/shard_map/ppermute | solution.py:23
  5.7 9.1 %collective-permute-start.7 = (bf16[64,512]{1,0:T(8,128)(2,1)}, bf16[64,512]{1,0:T(8,128)(2,1)S(1)}, u32[]{:S(2)}, u32[]{:S(2)}) collective-permute-start(bf16[64,512]{1,0:T(8,128)(2,1)} %refs_3_.5), channel_id=1, source_target_pairs={{0,2},{1,3},{2,0},{3,1},{4,6},{5,7},{6,4},{7,5},{8,10},{9,11},{10,... | collective-permute-start | bytes 196616 | tf_op jit(solution)/shard_map/ppermute | solution.py:23
  8.2 6.6 %collective-permute-start.2 = (bf16[64,512]{1,0:T(8,128)(2,1)S(1)}, bf16[64,512]{1,0:T(8,128)(2,1)S(1)}, u32[]{:S(2)}, u32[]{:S(2)}) collective-permute-start(bf16[64,512]{1,0:T(8,128)(2,1)S(1)} %collective-permute-done.1.refs_0_), channel_id=1, source_target_pairs={{0,2},{1,3},{2,0},{3,1},{4,6},{5,7},{6,4},{7,5},{8,10},{9,11},{10,... | collective-permute-start | bytes 196616 | tf_op jit(solution)/shard_map/ppermute | solution.py:23
  10.0 5.6 %collective-permute-start.4 = (bf16[64,512]{1,0:T(8,128)(2,1)S(1)}, bf16[64,512]{1,0:T(8,128)(2,1)S(1)}, u32[]{:S(2)}, u32[]{:S(2)}) collective-permute-start(bf16[64,512]{1,0:T(8,128)(2,1)S(1)} %collective-permute-done.3.refs_1_), channel_id=1, source_target_pairs={{0,2},{1,3},{2,0},{3,1},{4,6},{5,7},{6,4},{7,5},{8,10},{9,11},{10,... | collective-permute-start | bytes 196616 | tf_op jit(solution)/shard_map/ppermute | solution.py:23
  11.6 4.3 %collective-permute-start.6 = (bf16[64,512]{1,0:T(8,128)(2,1)S(1)}, bf16[64,512]{1,0:T(8,128)(2,1)S(1)}, u32[]{:S(2)}, u32[]{:S(2)}) collective-permute-start(bf16[64,512]{1,0:T(8,128)(2,1)S(1)} %collective-permute-done.5.refs_2_), channel_id=1, source_target_pairs={{0,2},{1,3},{2,0},{3,1},{4,6},{5,7},{6,4},{7,5},{8,10},{9,11},{10,... | collective-permute-start | bytes 196616 | tf_op jit(solution)/shard_map/ppermute | solution.py:23
  15.5 1.6 %collective-permute-start.9 = (bf16[4,64,512]{2,1,0:T(8,128)(2,1)S(1)}, bf16[4,64,512]{2,1,0:T(8,128)(2,1)S(1)}, u32[]{:S(2)}, u32[]{:S(2)}) collective-permute-start(bf16[4,64,512]{2,1,0:T(8,128)(2,1)S(1)} %join_column.1), channel_id=1, source_target_pairs={{0,1},{1,0},{2,3},{3,2},{4,5},{5,4},{6,7},{7,6},{8,9},{9,8},{10,11... | collective-permute-start | bytes 786440 | tf_op jit(solution)/shard_map/ppermute | solution.py:23
  15.9 1.7 %collective-permute-start.8 = (bf16[4,64,512]{2,1,0:T(8,128)(2,1)S(1)}, bf16[4,64,512]{2,1,0:T(8,128)(2,1)S(1)}, u32[]{:S(2)}, u32[]{:S(2)}) collective-permute-start(bf16[4,64,512]{2,1,0:T(8,128)(2,1)S(1)} %join_across.1), channel_id=1, source_target_pairs={{0,1},{1,0},{2,3},{3,2},{4,5},{5,4},{6,7},{7,6},{8,9},{9,8},{10,11... | collective-permute-start | bytes 786440 | tf_op jit(solution)/shard_map/ppermute | solution.py:23
  16.2 12.5 %collective-permute-start = (f32[8,4096]{1,0:T(8,128)S(1)}, f32[8,4096]{1,0:T(8,128)S(1)}, u32[]{:S(2)}, u32[]{:S(2)}) collective-permute-start(f32[8,4096]{1,0:T(8,128)S(1)} %get-tuple-element.20.targets), channel_id=1, source_target_pairs={{0,1},{1,0},{2,3},{3,2},{4,5},{5,4},{6,7},{7,6},{8,9},{9,8},{10,11... | collective-permute-start | bytes 393224 | tf_op jit(solution)/shard_map/ppermute | solution.py:23
  18.5 12.4 %slice-start = ((s8[33554432]{0:T(1024)(128)(4,1)}), s8[4194304]{0:T(1024)(128)(4,1)S(1)}, s32[]{:S(2)}) async-start(s8[33554432]{0:T(1024)(128)(4,1)} %bitcast.4), calls=%async_computation | async-start | bytes 8388608
  18.6 6.2 %collective-permute-start.10 = (bf16[4,16,256]{2,1,0:T(8,128)(2,1)S(1)}, bf16[4,16,256]{2,1,0:T(8,128)(2,1)S(1)}, u32[]{:S(2)}, u32[]{:S(2)}) collective-permute-start(bf16[4,16,256]{2,1,0:T(8,128)(2,1)S(1)} %hold_rows.1), channel_id=1, source_target_pairs={{0,12},{1,13},{2,14},{3,15},{4,8},{5,9},{6,10},{7,11},{8,4},{9,5},... | collective-permute-start | bytes 98312 | tf_op jit(solution)/shard_map/ppermute | solution.py:23
  21.9 4.8 %collective-permute-start.11 = (bf16[4,16,256]{2,1,0:T(8,128)(2,1)S(1)}, bf16[4,16,256]{2,1,0:T(8,128)(2,1)S(1)}, u32[]{:S(2)}, u32[]{:S(2)}) collective-permute-start(bf16[4,16,256]{2,1,0:T(8,128)(2,1)S(1)} %get-tuple-element.25), channel_id=1, source_target_pairs={{0,8},{1,9},{2,10},{3,11},{4,12},{5,13},{6,14},{7,15},{8,0},{9,1},... | collective-permute-start | bytes 98312 | tf_op jit(solution)/shard_map/ppermute | solution.py:23
  21.9 4.8 %collective-permute-start.12 = (bf16[4,16,256]{2,1,0:T(8,128)(2,1)S(1)}, bf16[4,16,256]{2,1,0:T(8,128)(2,1)S(1)}, u32[]{:S(2)}, u32[]{:S(2)}) collective-permute-start(bf16[4,16,256]{2,1,0:T(8,128)(2,1)S(1)} %get-tuple-element.26), channel_id=1, source_target_pairs={{0,4},{1,5},{2,6},{3,7},{4,0},{5,1},{6,2},{7,3},{8,12},{9,13},{10,... | collective-permute-start | bytes 98312 | tf_op jit(solution)/shard_map/ppermute | solution.py:23
  26.7 3.4 %collective-permute-start.13 = (bf16[4,16,256]{2,1,0:T(8,128)(2,1)S(1)}, bf16[4,16,256]{2,1,0:T(8,128)(2,1)S(1)}, u32[]{:S(2)}, u32[]{:S(2)}) collective-permute-start(bf16[4,16,256]{2,1,0:T(8,128)(2,1)S(1)} %get-tuple-element.28), channel_id=1, source_target_pairs={{0,3},{1,2},{2,1},{3,0},{4,7},{5,6},{6,5},{7,4},{8,11},{9,10},{10,... | collective-permute-start | bytes 98312 | tf_op jit(solution)/shard_map/ppermute | solution.py:23
  26.8 4.2 %collective-permute-start.14 = (bf16[4,16,256]{2,1,0:T(8,128)(2,1)S(1)}, bf16[4,16,256]{2,1,0:T(8,128)(2,1)S(1)}, u32[]{:S(2)}, u32[]{:S(2)}) collective-permute-start(bf16[4,16,256]{2,1,0:T(8,128)(2,1)S(1)} %get-tuple-element.29), channel_id=1, source_target_pairs={{0,2},{1,3},{2,0},{3,1},{4,6},{5,7},{6,4},{7,5},{8,10},{9,11},{10,... | collective-permute-start | bytes 98312 | tf_op jit(solution)/shard_map/ppermute | solution.py:23
  27.6 3.3 %collective-permute-start.15 = (bf16[4,16,256]{2,1,0:T(8,128)(2,1)S(1)}, bf16[4,16,256]{2,1,0:T(8,128)(2,1)S(1)}, u32[]{:S(2)}, u32[]{:S(2)}) collective-permute-start(bf16[4,16,256]{2,1,0:T(8,128)(2,1)S(1)} %get-tuple-element.30), channel_id=1, source_target_pairs={{0,1},{1,0},{2,3},{3,2},{4,5},{5,4},{6,7},{7,6},{8,9},{9,8},{10,11... | collective-permute-start | bytes 98312 | tf_op jit(solution)/shard_map/ppermute | solution.py:23
  35.5 1.3 %collective-permute-start.16 = (bf16[16,2048]{1,0:T(8,128)(2,1)S(1)}, bf16[16,2048]{1,0:T(8,128)(2,1)S(1)}, u32[]{:S(2)}, u32[]{:S(2)}) collective-permute-start(bf16[16,2048]{1,0:T(8,128)(2,1)S(1)} %get-tuple-element.32), channel_id=1, source_target_pairs={{0,1},{1,0},{2,3},{3,2},{4,5},{5,4},{6,7},{7,6},{8,9},{9,8},{10,11... | collective-permute-start | bytes 196616 | tf_op jit(solution)/shard_map/ppermute | solution.py:23
  36.8 5.8 %collective-permute-start.17 = (bf16[16,2048]{1,0:T(8,128)(2,1)S(1)}, bf16[16,2048]{1,0:T(8,128)(2,1)S(1)}, u32[]{:S(2)}, u32[]{:S(2)}) collective-permute-start(bf16[16,2048]{1,0:T(8,128)(2,1)S(1)} %fusion), channel_id=1, source_target_pairs={{0,6},{1,7},{2,4},{3,5},{4,2},{5,3},{6,0},{7,1},{8,14},{9,15},{10,... | collective-permute-start | bytes 196616 | tf_op jit(solution)/shard_map/ppermute | solution.py:23
  37.9 4.8 %collective-permute-start.18 = (bf16[16,2048]{1,0:T(8,128)(2,1)S(1)}, bf16[16,2048]{1,0:T(8,128)(2,1)S(1)}, u32[]{:S(2)}, u32[]{:S(2)}) collective-permute-start(bf16[16,2048]{1,0:T(8,128)(2,1)S(1)} %fusion), channel_id=1, source_target_pairs={{0,4},{1,5},{2,6},{3,7},{4,0},{5,1},{6,2},{7,3},{8,12},{9,13},{10,... | collective-permute-start | bytes 196616 | tf_op jit(solution)/shard_map/ppermute | solution.py:23
  38.9 4.4 %collective-permute-start.19 = (bf16[16,2048]{1,0:T(8,128)(2,1)S(1)}, bf16[16,2048]{1,0:T(8,128)(2,1)S(1)}, u32[]{:S(2)}, u32[]{:S(2)}) collective-permute-start(bf16[16,2048]{1,0:T(8,128)(2,1)S(1)} %fusion), channel_id=1, source_target_pairs={{0,2},{1,3},{2,0},{3,1},{4,6},{5,7},{6,4},{7,5},{8,10},{9,11},{10,... | collective-permute-start | bytes 196616 | tf_op jit(solution)/shard_map/ppermute | solution.py:23
  43.4 5.9 %collective-permute-start.20 = (bf16[16,2048]{1,0:T(8,128)(2,1)S(1)}, bf16[16,2048]{1,0:T(8,128)(2,1)S(1)}, u32[]{:S(2)}, u32[]{:S(2)}) collective-permute-start(bf16[16,2048]{1,0:T(8,128)(2,1)S(1)} %get-tuple-element.35), channel_id=1, source_target_pairs={{0,8},{1,9},{2,10},{3,11},{4,12},{5,13},{6,14},{7,15},{8,0},{9,1},... | collective-permute-start | bytes 196616 | tf_op jit(solution)/shard_map/ppermute | solution.py:23
  49.9 1.2 %collective-permute-start.21 = (f32[8,128]{1,0:T(8,128)S(1)}, f32[8,128]{1,0:T(8,128)S(1)}, u32[]{:S(2)}, u32[]{:S(2)}) collective-permute-start(f32[8,128]{1,0:T(8,128)S(1)} %get-tuple-element.34), channel_id=1, source_target_pairs={{0,1},{1,0},{2,3},{3,2},{4,5},{5,4},{6,7},{7,6},{8,9},{9,8},{10,11... | collective-permute-start | bytes 12296 | tf_op jit(solution)/shard_map/ppermute | solution.py:23
  (7 other events, 86.8 us)
where the time goes:
time: 51.9 us; the launch traced here: 51.7 us
  starting transfers between devices  24 us (46%)
  waiting for transfers between devices  16.9 us (33%)
  Pallas kernels  9.82 us (19%)
  other arithmetic  0.74 us (1%)
    ppermute x22, starting transfers between devices, swap(): return lax.ppermute(value, 'shard', [(s, s ^ bit) for s in range(n)])  24 us
    ppermute x22, waiting for transfers between devices, swap(): return lax.ppermute(value, 'shard', [(s, s ^ bit) for s in range(n)])  16.9 us
    pallas_call x1, Pallas kernels, partial_features(): pl.pallas_call(functools.partial(features_kernel, places, len(arrays)), o...  4.5 us
    pallas_call x1, Pallas kernels, load(): pl.pallas_call(functools.partial(load_kernel, len(parts), [start for _, s...  2.39 us
    pallas_call x3, Pallas kernels, partial_lowrank(): pl.pallas_call(functools.partial(lowrank_kernel, places), out_shape=jax.S...  1.34 us
  transfers between devices with their start and end apart: 22, of which 13 were waited for; matrix products, arithmetic and copies ran while one was open for 0% of the time, Pallas kernels for 9%

commit v1 on v0

--- a/solution.py
+++ b/solution.py
@@ -268,8 +268,9 @@
     rows = packed_grads(me, targets_of, tokens, other[1:], owners[1:], total, cotangent, mask)
     rows = list(rows)
     rows[-1] = hold("hold_rows", rows[-1], (), HIDE)
-    arrays = [swap(array, m, n) for array, m in zip(rows[:0:-1], moves[:0:-1])] + [rows[0]]
-    held = {(m, r): (a, i) for a, m in enumerate(moves[::-1]) for i, r in enumerate(left)}
+    turns = [len(moves) - 1] + list(range(1, len(moves) - 1)) + [0]
+    arrays = [swap(rows[a], moves[a], n) if a else rows[a] for a in turns]
+    held = {(moves[a], r): (place, i) for place, a in enumerate(turns) for i, r in enumerate(left)}
     for number, stage in enumerate(stages[1:]):
         moves, left = span(stage), span([b for later in stages[number + 2 :] for b in later])
         pairs = [[(src, r ^ m) for src in sorted({s for s, _ in held}) for r in left] for m in moves]

time: 51.9 us -> 51.7 us (level)
  starting transfers between devices: 24 us -> 23.4 us
    ppermute x22, starting transfers between devices: 24 us -> 23.4 us  [swap(): return lax.ppermute(value, 'shard', [(s, s ^ bit) for s in range(n)])]
  transfers between devices with their start and end apart: 22 -> 22, of which waited for: 13 -> 15; matrix products, arithmetic and copies ran while one was open for 0% -> 0% of each run, Pallas kernels for 9% -> 9%
where the time goes in v1:
time: 51.7 us; the launch traced here: 51.6 us
  starting transfers between devices  23.4 us (45%)
  waiting for transfers between devices  17.3 us (33%)
  Pallas kernels  9.82 us (19%)
  other arithmetic  0.74 us (1%)
    ppermute x22, starting transfers between devices, swap(): return lax.ppermute(value, 'shard', [(s, s ^ bit) for s in range(n)])  23.4 us
    ppermute x22, waiting for transfers between devices, swap(): return lax.ppermute(value, 'shard', [(s, s ^ bit) for s in range(n)])  17.3 us
    pallas_call x1, Pallas kernels, partial_features(): pl.pallas_call(functools.partial(features_kernel, places, len(arrays)), o...  4.5 us
    pallas_call x1, Pallas kernels, load(): pl.pallas_call(functools.partial(load_kernel, len(parts), [start for _, s...  2.39 us
    pallas_call x3, Pallas kernels, partial_lowrank(): pl.pallas_call(functools.partial(lowrank_kernel, places), out_shape=jax.S...  1.34 us
  transfers between devices with their start and end apart: 22, of which 15 were waited for; matrix products, arithmetic and copies ran while one was open for 0% of the time, Pallas kernels for 9%

profile of v1, /device:TPU:0, one launch (start us, length us, event | category | flops | bytes accessed | tf_op | source)
XLA Modules:
  0.0 51.6 jit_solution(17926638358748025220)
XLA Ops:
  0.0 5.0 %collective-permute-start.1 = (bf16[64,512]{1,0:T(8,128)(2,1)}, bf16[64,512]{1,0:T(8,128)(2,1)S(1)}, u32[]{:S(2)}, u32[]{:S(2)}) collective-permute-start(bf16[64,512]{1,0:T(8,128)(2,1)} %refs_3_.5), channel_id=1, source_target_pairs={{0,12},{1,13},{2,14},{3,15},{4,8},{5,9},{6,10},{7,11},{8,4},{9,5},... | collective-permute-start | bytes 196616 | tf_op jit(solution)/shard_map/ppermute | solution.py:23
  5.7 1.7 %collective-permute-start.7 = (bf16[64,512]{1,0:T(8,128)(2,1)}, bf16[64,512]{1,0:T(8,128)(2,1)S(1)}, u32[]{:S(2)}, u32[]{:S(2)}) collective-permute-start(bf16[64,512]{1,0:T(8,128)(2,1)} %refs_3_.5), channel_id=1, source_target_pairs={{0,2},{1,3},{2,0},{3,1},{4,6},{5,7},{6,4},{7,5},{8,10},{9,11},{10,... | collective-permute-start | bytes 196616 | tf_op jit(solution)/shard_map/ppermute | solution.py:23
  7.4 0.9 %collective-permute-done.1.refs_0_ = bf16[64,512]{1,0:T(8,128)(2,1)S(1)} collective-permute-done((bf16[64,512]{1,0:T(8,128)(2,1)}, bf16[64,512]{1,0:T(8,128)(2,1)S(1)}, u32[]{:S(2)}, u32[]{:S(2)}) %collective-permute-start.1) | collective-permute-done | bytes 65568 | tf_op jit(solution)/shard_map/ppermute | solution.py:23
  8.2 1.5 %collective-permute-start.2 = (bf16[64,512]{1,0:T(8,128)(2,1)S(1)}, bf16[64,512]{1,0:T(8,128)(2,1)S(1)}, u32[]{:S(2)}, u32[]{:S(2)}) collective-permute-start(bf16[64,512]{1,0:T(8,128)(2,1)S(1)} %collective-permute-done.1.refs_0_), channel_id=1, source_target_pairs={{0,2},{1,3},{2,0},{3,1},{4,6},{5,7},{6,4},{7,5},{8,10},{9,11},{10,... | collective-permute-start | bytes 196616 | tf_op jit(solution)/shard_map/ppermute | solution.py:23
  10.0 1.6 %collective-permute-start.4 = (bf16[64,512]{1,0:T(8,128)(2,1)S(1)}, bf16[64,512]{1,0:T(8,128)(2,1)S(1)}, u32[]{:S(2)}, u32[]{:S(2)}) collective-permute-start(bf16[64,512]{1,0:T(8,128)(2,1)S(1)} %collective-permute-done.3.refs_1_), channel_id=1, source_target_pairs={{0,2},{1,3},{2,0},{3,1},{4,6},{5,7},{6,4},{7,5},{8,10},{9,11},{10,... | collective-permute-start | bytes 196616 | tf_op jit(solution)/shard_map/ppermute | solution.py:23
  11.6 0.8 %collective-permute-start.6 = (bf16[64,512]{1,0:T(8,128)(2,1)S(1)}, bf16[64,512]{1,0:T(8,128)(2,1)S(1)}, u32[]{:S(2)}, u32[]{:S(2)}) collective-permute-start(bf16[64,512]{1,0:T(8,128)(2,1)S(1)} %collective-permute-done.5.refs_2_), channel_id=1, source_target_pairs={{0,2},{1,3},{2,0},{3,1},{4,6},{5,7},{6,4},{7,5},{8,10},{9,11},{10,... | collective-permute-start | bytes 196616 | tf_op jit(solution)/shard_map/ppermute | solution.py:23
  12.4 2.4 %load_1.1 = (bf16[256,8192]{1,0:T(8,128)(2,1)S(1)}, bf16[256,1024]{1,0:T(8,128)(2,1)S(1)}, s32[1,256]{1,0:T(1,128)S(1)}, f32[8,4096]{1,0:T(8,128)S(1)}) custom-call(bf16[256,8192]{1,0:T(8,128)(2,1)} %refs_0_.1, bf16[256,1024]{1,0:T(8,128)(2,1)} %refs_1_.1, s32[1,256]{1,0:T(1,128)} %bitcast.6, f32[8,4096]{1,0:T(8,128)} %refs_3_.3, s32[1]{0:T(128)} %bitcast.refs_4_.me), custom_call_target="tpu_custom_call" | custom-call | bytes 9701376 | tf_op jit(solution)/shard_map/load_1/pallas_call | solution.py:59
  17.5 1.0 %grads.1 = (bf16[4,16,256]{2,1,0:T(8,128)(2,1)S(1)}, bf16[4,16,256]{2,1,0:T(8,128)(2,1)S(1)}, bf16[4,16,256]{2,1,0:T(8,128)(2,1)S(1)}, bf16[4,16,256]{2,1,0:T(8,128)(2,1)S(1)}) custom-call(s32[1]{0:T(128)} %bitcast.refs_4_.me, bf16[256,8192]{1,0:T(8,128)(2,1)S(1)} %get-tuple-element.21.tokens, bf16[4,64,512]{2,1,0:T(8,128)(2,1)S(1)} %collective-permute-done.8.refs_0_, ...), custom_call_target="tpu_custom_call" | custom-call | flops 100000000 | bytes 2000000 | tf_op jit(solution)/shard_map/grads/pallas_call | solution.py:152
  18.6 3.2 %collective-permute-start.10 = (bf16[4,16,256]{2,1,0:T(8,128)(2,1)S(1)}, bf16[4,16,256]{2,1,0:T(8,128)(2,1)S(1)}, u32[]{:S(2)}, u32[]{:S(2)}) collective-permute-start(bf16[4,16,256]{2,1,0:T(8,128)(2,1)S(1)} %hold_rows.1), channel_id=1, source_target_pairs={{0,12},{1,13},{2,14},{3,15},{4,8},{5,9},{6,10},{7,11},{8,4},{9,5},... | collective-permute-start | bytes 98312 | tf_op jit(solution)/shard_map/ppermute | solution.py:23
  21.9 1.2 %collective-permute-start.12 = (bf16[4,16,256]{2,1,0:T(8,128)(2,1)S(1)}, bf16[4,16,256]{2,1,0:T(8,128)(2,1)S(1)}, u32[]{:S(2)}, u32[]{:S(2)}) collective-permute-start(bf16[4,16,256]{2,1,0:T(8,128)(2,1)S(1)} %get-tuple-element.26), channel_id=1, source_target_pairs={{0,8},{1,9},{2,10},{3,11},{4,12},{5,13},{6,14},{7,15},{8,0},{9,1},... | collective-permute-start | bytes 98312 | tf_op jit(solution)/shard_map/ppermute | solution.py:23
  23.1 1.3 %collective-permute-done.10.refs_0_.refs_3_ = bf16[4,16,256]{2,1,0:T(8,128)(2,1)S(1)} collective-permute-done((bf16[4,16,256]{2,1,0:T(8,128)(2,1)S(1)}, bf16[4,16,256]{2,1,0:T(8,128)(2,1)S(1)}, u32[]{:S(2)}, u32[]{:S(2)}) %collective-permute-start.10) | collective-permute-done | bytes 32800 | tf_op jit(solution)/shard_map/ppermute | solution.py:23
  24.4 1.5 %collective-permute-done.11.refs_1_.refs_4_ = bf16[4,16,256]{2,1,0:T(8,128)(2,1)S(1)} collective-permute-done((bf16[4,16,256]{2,1,0:T(8,128)(2,1)S(1)}, bf16[4,16,256]{2,1,0:T(8,128)(2,1)S(1)}, u32[]{:S(2)}, u32[]{:S(2)}) %collective-permute-start.11) | collective-permute-done | bytes 32800 | tf_op jit(solution)/shard_map/ppermute | solution.py:23
  25.9 1.1 %collective-permute-done.12.refs_2_.refs_5_ = bf16[4,16,256]{2,1,0:T(8,128)(2,1)S(1)} collective-permute-done((bf16[4,16,256]{2,1,0:T(8,128)(2,1)S(1)}, bf16[4,16,256]{2,1,0:T(8,128)(2,1)S(1)}, u32[]{:S(2)}, u32[]{:S(2)}) %collective-permute-start.12) | collective-permute-done | bytes 32800 | tf_op jit(solution)/shard_map/ppermute | solution.py:23
  27.9 1.0 %collective-permute-start.15 = (bf16[4,16,256]{2,1,0:T(8,128)(2,1)S(1)}, bf16[4,16,256]{2,1,0:T(8,128)(2,1)S(1)}, u32[]{:S(2)}, u32[]{:S(2)}) collective-permute-start(bf16[4,16,256]{2,1,0:T(8,128)(2,1)S(1)} %get-tuple-element.30), channel_id=1, source_target_pairs={{0,1},{1,0},{2,3},{3,2},{4,5},{5,4},{6,7},{7,6},{8,9},{9,8},{10,11... | collective-permute-start | bytes 98312 | tf_op jit(solution)/shard_map/ppermute | solution.py:23
  29.0 1.5 %collective-permute-done.13.refs_0_ = bf16[4,16,256]{2,1,0:T(8,128)(2,1)S(1)} collective-permute-done((bf16[4,16,256]{2,1,0:T(8,128)(2,1)S(1)}, bf16[4,16,256]{2,1,0:T(8,128)(2,1)S(1)}, u32[]{:S(2)}, u32[]{:S(2)}) %collective-permute-start.13) | collective-permute-done | bytes 32800 | tf_op jit(solution)/shard_map/ppermute | solution.py:23
  30.4 0.8 %collective-permute-done.14.refs_1_ = bf16[4,16,256]{2,1,0:T(8,128)(2,1)S(1)} collective-permute-done((bf16[4,16,256]{2,1,0:T(8,128)(2,1)S(1)}, bf16[4,16,256]{2,1,0:T(8,128)(2,1)S(1)}, u32[]{:S(2)}, u32[]{:S(2)}) %collective-permute-start.14) | collective-permute-done | bytes 32800 | tf_op jit(solution)/shard_map/ppermute | solution.py:23
  31.4 4.5 %features.1 = (f32[16,2048]{1,0:T(8,128)S(1)}, bf16[16,2048]{1,0:T(8,128)(2,1)S(1)}) custom-call(s32[1]{0:T(128)} %bitcast.refs_4_.me, bf16[4,16,256]{2,1,0:T(8,128)(2,1)S(1)} %collective-permute-done.13.refs_0_, bf16[4,16,256]{2,1,0:T(8,128)(2,1)S(1)} %collective-permute-done.14.refs_1_, bf16[4,16,256]{2,1,0:T(8,128)(2,1)S(1)} %collective-permute-done.15.refs_2_, ...), custom_call_target="tpu_custom_call" | custom-call | flops 600000000 | bytes 34000000 | tf_op jit(solution)/shard_map/features/pallas_call | solution.py:192
  35.9 1.2 %collective-permute-done.16 = bf16[16,2048]{1,0:T(8,128)(2,1)S(1)} collective-permute-done((bf16[16,2048]{1,0:T(8,128)(2,1)S(1)}, bf16[16,2048]{1,0:T(8,128)(2,1)S(1)}, u32[]{:S(2)}, u32[]{:S(2)}) %collective-permute-start.16) | collective-permute-done | bytes 65568 | tf_op jit(solution)/shard_map/ppermute | solution.py:23
  37.1 1.8 %collective-permute-start.17 = (bf16[16,2048]{1,0:T(8,128)(2,1)S(1)}, bf16[16,2048]{1,0:T(8,128)(2,1)S(1)}, u32[]{:S(2)}, u32[]{:S(2)}) collective-permute-start(bf16[16,2048]{1,0:T(8,128)(2,1)S(1)} %fusion), channel_id=1, source_target_pairs={{0,6},{1,7},{2,4},{3,5},{4,2},{5,3},{6,0},{7,1},{8,14},{9,15},{10,... | collective-permute-start | bytes 196616 | tf_op jit(solution)/shard_map/ppermute | solution.py:23
  39.3 1.4 %collective-permute-start.19 = (bf16[16,2048]{1,0:T(8,128)(2,1)S(1)}, bf16[16,2048]{1,0:T(8,128)(2,1)S(1)}, u32[]{:S(2)}, u32[]{:S(2)}) collective-permute-start(bf16[16,2048]{1,0:T(8,128)(2,1)S(1)} %fusion), channel_id=1, source_target_pairs={{0,2},{1,3},{2,0},{3,1},{4,6},{5,7},{6,4},{7,5},{8,10},{9,11},{10,... | collective-permute-start | bytes 196616 | tf_op jit(solution)/shard_map/ppermute | solution.py:23
  40.7 1.9 %collective-permute-done.17 = bf16[16,2048]{1,0:T(8,128)(2,1)S(1)} collective-permute-done((bf16[16,2048]{1,0:T(8,128)(2,1)S(1)}, bf16[16,2048]{1,0:T(8,128)(2,1)S(1)}, u32[]{:S(2)}, u32[]{:S(2)}) %collective-permute-start.17) | collective-permute-done | bytes 65568 | tf_op jit(solution)/shard_map/ppermute | solution.py:23
  43.7 1.5 %collective-permute-start.20 = (bf16[16,2048]{1,0:T(8,128)(2,1)S(1)}, bf16[16,2048]{1,0:T(8,128)(2,1)S(1)}, u32[]{:S(2)}, u32[]{:S(2)}) collective-permute-start(bf16[16,2048]{1,0:T(8,128)(2,1)S(1)} %get-tuple-element.35), channel_id=1, source_target_pairs={{0,8},{1,9},{2,10},{3,11},{4,12},{5,13},{6,14},{7,15},{8,0},{9,1},... | collective-permute-start | bytes 196616 | tf_op jit(solution)/shard_map/ppermute | solution.py:23
  45.2 3.9 %collective-permute-done.20.refs_0_ = bf16[16,2048]{1,0:T(8,128)(2,1)S(1)} collective-permute-done((bf16[16,2048]{1,0:T(8,128)(2,1)S(1)}, bf16[16,2048]{1,0:T(8,128)(2,1)S(1)}, u32[]{:S(2)}, u32[]{:S(2)}) %collective-permute-start.20) | collective-permute-done | bytes 65568 | tf_op jit(solution)/shard_map/ppermute | solution.py:23
  49.7 1.2 %collective-permute-done.21 = f32[8,128]{1,0:T(8,128)S(1)} collective-permute-done((f32[8,128]{1,0:T(8,128)S(1)}, f32[8,128]{1,0:T(8,128)S(1)}, u32[]{:S(2)}, u32[]{:S(2)}) %collective-permute-start.21) | collective-permute-done | bytes 4128 | tf_op jit(solution)/shard_map/ppermute | solution.py:23
  (54 shorter events, 7.2 us)
Async XLA Ops:
  0.0 14.8 %copy-start = (bf16[64,512]{1,0:T(8,128)(2,1)S(1)}, bf16[64,512]{1,0:T(8,128)(2,1)}, u32[]{:S(2)}) copy-start(bf16[64,512]{1,0:T(8,128)(2,1)} %refs_3_.5) | copy-start | bytes 196612
  0.0 8.2 %collective-permute-start.1 = (bf16[64,512]{1,0:T(8,128)(2,1)}, bf16[64,512]{1,0:T(8,128)(2,1)S(1)}, u32[]{:S(2)}, u32[]{:S(2)}) collective-permute-start(bf16[64,512]{1,0:T(8,128)(2,1)} %refs_3_.5), channel_id=1, source_target_pairs={{0,12},{1,13},{2,14},{3,15},{4,8},{5,9},{6,10},{7,11},{8,4},{9,5},... | collective-permute-start | bytes 196616 | tf_op jit(solution)/shard_map/ppermute | solution.py:23
  5.1 4.9 %collective-permute-start.3 = (bf16[64,512]{1,0:T(8,128)(2,1)}, bf16[64,512]{1,0:T(8,128)(2,1)S(1)}, u32[]{:S(2)}, u32[]{:S(2)}) collective-permute-start(bf16[64,512]{1,0:T(8,128)(2,1)} %refs_3_.5), channel_id=1, source_target_pairs={{0,4},{1,5},{2,6},{3,7},{4,0},{5,1},{6,2},{7,3},{8,12},{9,13},{10,... | collective-permute-start | bytes 196616 | tf_op jit(solution)/shard_map/ppermute | solution.py:23
  5.1 6.5 %collective-permute-start.5 = (bf16[64,512]{1,0:T(8,128)(2,1)}, bf16[64,512]{1,0:T(8,128)(2,1)S(1)}, u32[]{:S(2)}, u32[]{:S(2)}) collective-permute-start(bf16[64,512]{1,0:T(8,128)(2,1)} %refs_3_.5), channel_id=1, source_target_pairs={{0,8},{1,9},{2,10},{3,11},{4,12},{5,13},{6,14},{7,15},{8,0},{9,1},... | collective-permute-start | bytes 196616 | tf_op jit(solution)/shard_map/ppermute | solution.py:23
  5.7 9.1 %collective-permute-start.7 = (bf16[64,512]{1,0:T(8,128)(2,1)}, bf16[64,512]{1,0:T(8,128)(2,1)S(1)}, u32[]{:S(2)}, u32[]{:S(2)}) collective-permute-start(bf16[64,512]{1,0:T(8,128)(2,1)} %refs_3_.5), channel_id=1, source_target_pairs={{0,2},{1,3},{2,0},{3,1},{4,6},{5,7},{6,4},{7,5},{8,10},{9,11},{10,... | collective-permute-start | bytes 196616 | tf_op jit(solution)/shard_map/ppermute | solution.py:23
  8.2 6.6 %collective-permute-start.2 = (bf16[64,512]{1,0:T(8,128)(2,1)S(1)}, bf16[64,512]{1,0:T(8,128)(2,1)S(1)}, u32[]{:S(2)}, u32[]{:S(2)}) collective-permute-start(bf16[64,512]{1,0:T(8,128)(2,1)S(1)} %collective-permute-done.1.refs_0_), channel_id=1, source_target_pairs={{0,2},{1,3},{2,0},{3,1},{4,6},{5,7},{6,4},{7,5},{8,10},{9,11},{10,... | collective-permute-start | bytes 196616 | tf_op jit(solution)/shard_map/ppermute | solution.py:23
  10.0 5.6 %collective-permute-start.4 = (bf16[64,512]{1,0:T(8,128)(2,1)S(1)}, bf16[64,512]{1,0:T(8,128)(2,1)S(1)}, u32[]{:S(2)}, u32[]{:S(2)}) collective-permute-start(bf16[64,512]{1,0:T(8,128)(2,1)S(1)} %collective-permute-done.3.refs_1_), channel_id=1, source_target_pairs={{0,2},{1,3},{2,0},{3,1},{4,6},{5,7},{6,4},{7,5},{8,10},{9,11},{10,... | collective-permute-start | bytes 196616 | tf_op jit(solution)/shard_map/ppermute | solution.py:23
  11.6 4.3 %collective-permute-start.6 = (bf16[64,512]{1,0:T(8,128)(2,1)S(1)}, bf16[64,512]{1,0:T(8,128)(2,1)S(1)}, u32[]{:S(2)}, u32[]{:S(2)}) collective-permute-start(bf16[64,512]{1,0:T(8,128)(2,1)S(1)} %collective-permute-done.5.refs_2_), channel_id=1, source_target_pairs={{0,2},{1,3},{2,0},{3,1},{4,6},{5,7},{6,4},{7,5},{8,10},{9,11},{10,... | collective-permute-start | bytes 196616 | tf_op jit(solution)/shard_map/ppermute | solution.py:23
  15.5 1.6 %collective-permute-start.9 = (bf16[4,64,512]{2,1,0:T(8,128)(2,1)S(1)}, bf16[4,64,512]{2,1,0:T(8,128)(2,1)S(1)}, u32[]{:S(2)}, u32[]{:S(2)}) collective-permute-start(bf16[4,64,512]{2,1,0:T(8,128)(2,1)S(1)} %join_column.1), channel_id=1, source_target_pairs={{0,1},{1,0},{2,3},{3,2},{4,5},{5,4},{6,7},{7,6},{8,9},{9,8},{10,11... | collective-permute-start | bytes 786440 | tf_op jit(solution)/shard_map/ppermute | solution.py:23
  15.9 1.7 %collective-permute-start.8 = (bf16[4,64,512]{2,1,0:T(8,128)(2,1)S(1)}, bf16[4,64,512]{2,1,0:T(8,128)(2,1)S(1)}, u32[]{:S(2)}, u32[]{:S(2)}) collective-permute-start(bf16[4,64,512]{2,1,0:T(8,128)(2,1)S(1)} %join_across.1), channel_id=1, source_target_pairs={{0,1},{1,0},{2,3},{3,2},{4,5},{5,4},{6,7},{7,6},{8,9},{9,8},{10,11... | collective-permute-start | bytes 786440 | tf_op jit(solution)/shard_map/ppermute | solution.py:23
  16.2 12.8 %collective-permute-start = (f32[8,4096]{1,0:T(8,128)S(1)}, f32[8,4096]{1,0:T(8,128)S(1)}, u32[]{:S(2)}, u32[]{:S(2)}) collective-permute-start(f32[8,4096]{1,0:T(8,128)S(1)} %get-tuple-element.20.targets), channel_id=1, source_target_pairs={{0,1},{1,0},{2,3},{3,2},{4,5},{5,4},{6,7},{7,6},{8,9},{9,8},{10,11... | collective-permute-start | bytes 393224 | tf_op jit(solution)/shard_map/ppermute | solution.py:23
  18.5 12.8 %slice-start = ((s8[33554432]{0:T(1024)(128)(4,1)}), s8[4194304]{0:T(1024)(128)(4,1)S(1)}, s32[]{:S(2)}) async-start(s8[33554432]{0:T(1024)(128)(4,1)} %bitcast.4), calls=%async_computation | async-start | bytes 8388608
  18.6 5.8 %collective-permute-start.10 = (bf16[4,16,256]{2,1,0:T(8,128)(2,1)S(1)}, bf16[4,16,256]{2,1,0:T(8,128)(2,1)S(1)}, u32[]{:S(2)}, u32[]{:S(2)}) collective-permute-start(bf16[4,16,256]{2,1,0:T(8,128)(2,1)S(1)} %hold_rows.1), channel_id=1, source_target_pairs={{0,12},{1,13},{2,14},{3,15},{4,8},{5,9},{6,10},{7,11},{8,4},{9,5},... | collective-permute-start | bytes 98312 | tf_op jit(solution)/shard_map/ppermute | solution.py:23
  21.9 4.1 %collective-permute-start.11 = (bf16[4,16,256]{2,1,0:T(8,128)(2,1)S(1)}, bf16[4,16,256]{2,1,0:T(8,128)(2,1)S(1)}, u32[]{:S(2)}, u32[]{:S(2)}) collective-permute-start(bf16[4,16,256]{2,1,0:T(8,128)(2,1)S(1)} %get-tuple-element.25), channel_id=1, source_target_pairs={{0,4},{1,5},{2,6},{3,7},{4,0},{5,1},{6,2},{7,3},{8,12},{9,13},{10,... | collective-permute-start | bytes 98312 | tf_op jit(solution)/shard_map/ppermute | solution.py:23
  21.9 5.2 %collective-permute-start.12 = (bf16[4,16,256]{2,1,0:T(8,128)(2,1)S(1)}, bf16[4,16,256]{2,1,0:T(8,128)(2,1)S(1)}, u32[]{:S(2)}, u32[]{:S(2)}) collective-permute-start(bf16[4,16,256]{2,1,0:T(8,128)(2,1)S(1)} %get-tuple-element.26), channel_id=1, source_target_pairs={{0,8},{1,9},{2,10},{3,11},{4,12},{5,13},{6,14},{7,15},{8,0},{9,1},... | collective-permute-start | bytes 98312 | tf_op jit(solution)/shard_map/ppermute | solution.py:23
  27.0 3.4 %collective-permute-start.13 = (bf16[4,16,256]{2,1,0:T(8,128)(2,1)S(1)}, bf16[4,16,256]{2,1,0:T(8,128)(2,1)S(1)}, u32[]{:S(2)}, u32[]{:S(2)}) collective-permute-start(bf16[4,16,256]{2,1,0:T(8,128)(2,1)S(1)} %get-tuple-element.28), channel_id=1, source_target_pairs={{0,3},{1,2},{2,1},{3,0},{4,7},{5,6},{6,5},{7,4},{8,11},{9,10},{10,... | collective-permute-start | bytes 98312 | tf_op jit(solution)/shard_map/ppermute | solution.py:23
  27.1 4.2 %collective-permute-start.14 = (bf16[4,16,256]{2,1,0:T(8,128)(2,1)S(1)}, bf16[4,16,256]{2,1,0:T(8,128)(2,1)S(1)}, u32[]{:S(2)}, u32[]{:S(2)}) collective-permute-start(bf16[4,16,256]{2,1,0:T(8,128)(2,1)S(1)} %get-tuple-element.29), channel_id=1, source_target_pairs={{0,2},{1,3},{2,0},{3,1},{4,6},{5,7},{6,4},{7,5},{8,10},{9,11},{10,... | collective-permute-start | bytes 98312 | tf_op jit(solution)/shard_map/ppermute | solution.py:23
  27.9 3.3 %collective-permute-start.15 = (bf16[4,16,256]{2,1,0:T(8,128)(2,1)S(1)}, bf16[4,16,256]{2,1,0:T(8,128)(2,1)S(1)}, u32[]{:S(2)}, u32[]{:S(2)}) collective-permute-start(bf16[4,16,256]{2,1,0:T(8,128)(2,1)S(1)} %get-tuple-element.30), channel_id=1, source_target_pairs={{0,1},{1,0},{2,3},{3,2},{4,5},{5,4},{6,7},{7,6},{8,9},{9,8},{10,11... | collective-permute-start | bytes 98312 | tf_op jit(solution)/shard_map/ppermute | solution.py:23
  35.9 1.3 %collective-permute-start.16 = (bf16[16,2048]{1,0:T(8,128)(2,1)S(1)}, bf16[16,2048]{1,0:T(8,128)(2,1)S(1)}, u32[]{:S(2)}, u32[]{:S(2)}) collective-permute-start(bf16[16,2048]{1,0:T(8,128)(2,1)S(1)} %get-tuple-element.32), channel_id=1, source_target_pairs={{0,1},{1,0},{2,3},{3,2},{4,5},{5,4},{6,7},{7,6},{8,9},{9,8},{10,11... | collective-permute-start | bytes 196616 | tf_op jit(solution)/shard_map/ppermute | solution.py:23
  37.1 5.4 %collective-permute-start.17 = (bf16[16,2048]{1,0:T(8,128)(2,1)S(1)}, bf16[16,2048]{1,0:T(8,128)(2,1)S(1)}, u32[]{:S(2)}, u32[]{:S(2)}) collective-permute-start(bf16[16,2048]{1,0:T(8,128)(2,1)S(1)} %fusion), channel_id=1, source_target_pairs={{0,6},{1,7},{2,4},{3,5},{4,2},{5,3},{6,0},{7,1},{8,14},{9,15},{10,... | collective-permute-start | bytes 196616 | tf_op jit(solution)/shard_map/ppermute | solution.py:23
  38.9 4.3 %collective-permute-start.18 = (bf16[16,2048]{1,0:T(8,128)(2,1)S(1)}, bf16[16,2048]{1,0:T(8,128)(2,1)S(1)}, u32[]{:S(2)}, u32[]{:S(2)}) collective-permute-start(bf16[16,2048]{1,0:T(8,128)(2,1)S(1)} %fusion), channel_id=1, source_target_pairs={{0,4},{1,5},{2,6},{3,7},{4,0},{5,1},{6,2},{7,3},{8,12},{9,13},{10,... | collective-permute-start | bytes 196616 | tf_op jit(solution)/shard_map/ppermute | solution.py:23
  39.3 4.4 %collective-permute-start.19 = (bf16[16,2048]{1,0:T(8,128)(2,1)S(1)}, bf16[16,2048]{1,0:T(8,128)(2,1)S(1)}, u32[]{:S(2)}, u32[]{:S(2)}) collective-permute-start(bf16[16,2048]{1,0:T(8,128)(2,1)S(1)} %fusion), channel_id=1, source_target_pairs={{0,2},{1,3},{2,0},{3,1},{4,6},{5,7},{6,4},{7,5},{8,10},{9,11},{10,... | collective-permute-start | bytes 196616 | tf_op jit(solution)/shard_map/ppermute | solution.py:23
  43.7 5.4 %collective-permute-start.20 = (bf16[16,2048]{1,0:T(8,128)(2,1)S(1)}, bf16[16,2048]{1,0:T(8,128)(2,1)S(1)}, u32[]{:S(2)}, u32[]{:S(2)}) collective-permute-start(bf16[16,2048]{1,0:T(8,128)(2,1)S(1)} %get-tuple-element.35), channel_id=1, source_target_pairs={{0,8},{1,9},{2,10},{3,11},{4,12},{5,13},{6,14},{7,15},{8,0},{9,1},... | collective-permute-start | bytes 196616 | tf_op jit(solution)/shard_map/ppermute | solution.py:23
  49.7 1.2 %collective-permute-start.21 = (f32[8,128]{1,0:T(8,128)S(1)}, f32[8,128]{1,0:T(8,128)S(1)}, u32[]{:S(2)}, u32[]{:S(2)}) collective-permute-start(f32[8,128]{1,0:T(8,128)S(1)} %get-tuple-element.34), channel_id=1, source_target_pairs={{0,1},{1,0},{2,3},{3,2},{4,5},{5,4},{6,7},{7,6},{8,9},{9,8},{10,11... | collective-permute-start | bytes 12296 | tf_op jit(solution)/shard_map/ppermute | solution.py:23
  (7 other events, 89.3 us)

commit v2 on v0

--- a/solution.py
+++ b/solution.py
@@ -43,7 +43,7 @@
     copies = []
     for source, start, out in zip(sources, starts, outs):
         rows = out.shape[0]
-        step = min(rows, LANES // 2)
+        step = min(rows, LANES // 8)
         for i in range(0, rows, step):
             part = source.at[pl.ds(start + i, step)]
             copies.append(pltpu.make_async_copy(part, out.at[pl.ds(i, step)], sems.at[len(copies)]))
@@ -55,7 +55,7 @@
 
 def load(name, parts, after):
     size = sum(rows * array.size // array.shape[0] * array.dtype.itemsize for array, _, rows in parts)
-    pieces = sum(max(rows // (LANES // 2), 1) for _, _, rows in parts)
+    pieces = sum(max(rows // (LANES // 8), 1) for _, _, rows in parts)
     return pl.pallas_call(
         functools.partial(load_kernel, len(parts), [start for _, start, _ in parts]),
         out_shape=[pltpu.VMEM((rows,) + array.shape[1:], array.dtype) for array, _, rows in parts],

time: 51.9 us -> 51.9 us (level)
  no operation moved by 1% of the time
where the time goes in v2:
time: 51.9 us; the launch traced here: 51.7 us
  starting transfers between devices  24 us (46%)
  waiting for transfers between devices  16.8 us (32%)
  Pallas kernels  9.9 us (19%)
  other arithmetic  0.74 us (1%)
    ppermute x22, starting transfers between devices, swap(): return lax.ppermute(value, 'shard', [(s, s ^ bit) for s in range(n)])  24 us
    ppermute x22, waiting for transfers between devices, swap(): return lax.ppermute(value, 'shard', [(s, s ^ bit) for s in range(n)])  16.8 us
    pallas_call x1, Pallas kernels, partial_features(): pl.pallas_call(functools.partial(features_kernel, places, len(arrays)), o...  4.5 us
    pallas_call x1, Pallas kernels, load(): pl.pallas_call(functools.partial(load_kernel, len(parts), [start for _, s...  2.48 us
    pallas_call x3, Pallas kernels, partial_lowrank(): pl.pallas_call(functools.partial(lowrank_kernel, places), out_shape=jax.S...  1.34 us
  transfers between devices with their start and end apart: 22, of which 13 were waited for; matrix products, arithmetic and copies ran while one was open for 0% of the time, Pallas kernels for 9%

profile of v2, /device:TPU:0, one launch (start us, length us, event | category | flops | bytes accessed | tf_op | source)
XLA Modules:
  0.0 51.7 jit_solution(10026082958505791994)
XLA Ops:
  0.0 5.0 %collective-permute-start.1 = (bf16[64,512]{1,0:T(8,128)(2,1)}, bf16[64,512]{1,0:T(8,128)(2,1)S(1)}, u32[]{:S(2)}, u32[]{:S(2)}) collective-permute-start(bf16[64,512]{1,0:T(8,128)(2,1)} %refs_3_.5), channel_id=1, source_target_pairs={{0,12},{1,13},{2,14},{3,15},{4,8},{5,9},{6,10},{7,11},{8,4},{9,5},... | collective-permute-start | bytes 196616 | tf_op jit(solution)/shard_map/ppermute | solution.py:23
  5.7 1.7 %collective-permute-start.7 = (bf16[64,512]{1,0:T(8,128)(2,1)}, bf16[64,512]{1,0:T(8,128)(2,1)S(1)}, u32[]{:S(2)}, u32[]{:S(2)}) collective-permute-start(bf16[64,512]{1,0:T(8,128)(2,1)} %refs_3_.5), channel_id=1, source_target_pairs={{0,2},{1,3},{2,0},{3,1},{4,6},{5,7},{6,4},{7,5},{8,10},{9,11},{10,... | collective-permute-start | bytes 196616 | tf_op jit(solution)/shard_map/ppermute | solution.py:23
  7.4 0.9 %collective-permute-done.1.refs_0_ = bf16[64,512]{1,0:T(8,128)(2,1)S(1)} collective-permute-done((bf16[64,512]{1,0:T(8,128)(2,1)}, bf16[64,512]{1,0:T(8,128)(2,1)S(1)}, u32[]{:S(2)}, u32[]{:S(2)}) %collective-permute-start.1) | collective-permute-done | bytes 65568 | tf_op jit(solution)/shard_map/ppermute | solution.py:23
  8.2 1.5 %collective-permute-start.2 = (bf16[64,512]{1,0:T(8,128)(2,1)S(1)}, bf16[64,512]{1,0:T(8,128)(2,1)S(1)}, u32[]{:S(2)}, u32[]{:S(2)}) collective-permute-start(bf16[64,512]{1,0:T(8,128)(2,1)S(1)} %collective-permute-done.1.refs_0_), channel_id=1, source_target_pairs={{0,2},{1,3},{2,0},{3,1},{4,6},{5,7},{6,4},{7,5},{8,10},{9,11},{10,... | collective-permute-start | bytes 196616 | tf_op jit(solution)/shard_map/ppermute | solution.py:23
  10.0 1.6 %collective-permute-start.4 = (bf16[64,512]{1,0:T(8,128)(2,1)S(1)}, bf16[64,512]{1,0:T(8,128)(2,1)S(1)}, u32[]{:S(2)}, u32[]{:S(2)}) collective-permute-start(bf16[64,512]{1,0:T(8,128)(2,1)S(1)} %collective-permute-done.3.refs_1_), channel_id=1, source_target_pairs={{0,2},{1,3},{2,0},{3,1},{4,6},{5,7},{6,4},{7,5},{8,10},{9,11},{10,... | collective-permute-start | bytes 196616 | tf_op jit(solution)/shard_map/ppermute | solution.py:23
  11.6 0.8 %collective-permute-start.6 = (bf16[64,512]{1,0:T(8,128)(2,1)S(1)}, bf16[64,512]{1,0:T(8,128)(2,1)S(1)}, u32[]{:S(2)}, u32[]{:S(2)}) collective-permute-start(bf16[64,512]{1,0:T(8,128)(2,1)S(1)} %collective-permute-done.5.refs_2_), channel_id=1, source_target_pairs={{0,2},{1,3},{2,0},{3,1},{4,6},{5,7},{6,4},{7,5},{8,10},{9,11},{10,... | collective-permute-start | bytes 196616 | tf_op jit(solution)/shard_map/ppermute | solution.py:23
  12.4 2.5 %load_1.1 = (bf16[256,8192]{1,0:T(8,128)(2,1)S(1)}, bf16[256,1024]{1,0:T(8,128)(2,1)S(1)}, s32[1,256]{1,0:T(1,128)S(1)}, f32[8,4096]{1,0:T(8,128)S(1)}) custom-call(bf16[256,8192]{1,0:T(8,128)(2,1)} %refs_0_.1, bf16[256,1024]{1,0:T(8,128)(2,1)} %refs_1_.1, s32[1,256]{1,0:T(1,128)} %bitcast.6, f32[8,4096]{1,0:T(8,128)} %refs_3_.3, s32[1]{0:T(128)} %bitcast.refs_4_.me), custom_call_target="tpu_custom_call" | custom-call | bytes 9701376 | tf_op jit(solution)/shard_map/load_1/pallas_call | solution.py:59
  17.6 1.0 %grads.1 = (bf16[4,16,256]{2,1,0:T(8,128)(2,1)S(1)}, bf16[4,16,256]{2,1,0:T(8,128)(2,1)S(1)}, bf16[4,16,256]{2,1,0:T(8,128)(2,1)S(1)}, bf16[4,16,256]{2,1,0:T(8,128)(2,1)S(1)}) custom-call(s32[1]{0:T(128)} %bitcast.refs_4_.me, bf16[256,8192]{1,0:T(8,128)(2,1)S(1)} %get-tuple-element.21.tokens, bf16[4,64,512]{2,1,0:T(8,128)(2,1)S(1)} %collective-permute-done.8.refs_0_, ...), custom_call_target="tpu_custom_call" | custom-call | flops 100000000 | bytes 2000000 | tf_op jit(solution)/shard_map/grads/pallas_call | solution.py:152
  18.7 3.3 %collective-permute-start.10 = (bf16[4,16,256]{2,1,0:T(8,128)(2,1)S(1)}, bf16[4,16,256]{2,1,0:T(8,128)(2,1)S(1)}, u32[]{:S(2)}, u32[]{:S(2)}) collective-permute-start(bf16[4,16,256]{2,1,0:T(8,128)(2,1)S(1)} %hold_rows.1), channel_id=1, source_target_pairs={{0,12},{1,13},{2,14},{3,15},{4,8},{5,9},{6,10},{7,11},{8,4},{9,5},... | collective-permute-start | bytes 98312 | tf_op jit(solution)/shard_map/ppermute | solution.py:23
  21.9 1.2 %collective-permute-start.12 = (bf16[4,16,256]{2,1,0:T(8,128)(2,1)S(1)}, bf16[4,16,256]{2,1,0:T(8,128)(2,1)S(1)}, u32[]{:S(2)}, u32[]{:S(2)}) collective-permute-start(bf16[4,16,256]{2,1,0:T(8,128)(2,1)S(1)} %get-tuple-element.26), channel_id=1, source_target_pairs={{0,4},{1,5},{2,6},{3,7},{4,0},{5,1},{6,2},{7,3},{8,12},{9,13},{10,... | collective-permute-start | bytes 98312 | tf_op jit(solution)/shard_map/ppermute | solution.py:23
  23.1 1.7 %collective-permute-done.10.refs_0_.refs_3_ = bf16[4,16,256]{2,1,0:T(8,128)(2,1)S(1)} collective-permute-done((bf16[4,16,256]{2,1,0:T(8,128)(2,1)S(1)}, bf16[4,16,256]{2,1,0:T(8,128)(2,1)S(1)}, u32[]{:S(2)}, u32[]{:S(2)}) %collective-permute-start.10) | collective-permute-done | bytes 32800 | tf_op jit(solution)/shard_map/ppermute | solution.py:23
  24.9 1.9 %collective-permute-done.11.refs_1_.refs_4_ = bf16[4,16,256]{2,1,0:T(8,128)(2,1)S(1)} collective-permute-done((bf16[4,16,256]{2,1,0:T(8,128)(2,1)S(1)}, bf16[4,16,256]{2,1,0:T(8,128)(2,1)S(1)}, u32[]{:S(2)}, u32[]{:S(2)}) %collective-permute-start.11) | collective-permute-done | bytes 32800 | tf_op jit(solution)/shard_map/ppermute | solution.py:23
  27.6 1.1 %collective-permute-start.15 = (bf16[4,16,256]{2,1,0:T(8,128)(2,1)S(1)}, bf16[4,16,256]{2,1,0:T(8,128)(2,1)S(1)}, u32[]{:S(2)}, u32[]{:S(2)}) collective-permute-start(bf16[4,16,256]{2,1,0:T(8,128)(2,1)S(1)} %get-tuple-element.30), channel_id=1, source_target_pairs={{0,1},{1,0},{2,3},{3,2},{4,5},{5,4},{6,7},{7,6},{8,9},{9,8},{10,11... | collective-permute-start | bytes 98312 | tf_op jit(solution)/shard_map/ppermute | solution.py:23
  28.7 1.5 %collective-permute-done.13.refs_0_ = bf16[4,16,256]{2,1,0:T(8,128)(2,1)S(1)} collective-permute-done((bf16[4,16,256]{2,1,0:T(8,128)(2,1)S(1)}, bf16[4,16,256]{2,1,0:T(8,128)(2,1)S(1)}, u32[]{:S(2)}, u32[]{:S(2)}) %collective-permute-start.13) | collective-permute-done | bytes 32800 | tf_op jit(solution)/shard_map/ppermute | solution.py:23
  30.2 0.7 %collective-permute-done.14.refs_1_ = bf16[4,16,256]{2,1,0:T(8,128)(2,1)S(1)} collective-permute-done((bf16[4,16,256]{2,1,0:T(8,128)(2,1)S(1)}, bf16[4,16,256]{2,1,0:T(8,128)(2,1)S(1)}, u32[]{:S(2)}, u32[]{:S(2)}) %collective-permute-start.14) | collective-permute-done | bytes 32800 | tf_op jit(solution)/shard_map/ppermute | solution.py:23
  31.0 4.5 %features.1 = (f32[16,2048]{1,0:T(8,128)S(1)}, bf16[16,2048]{1,0:T(8,128)(2,1)S(1)}) custom-call(s32[1]{0:T(128)} %bitcast.refs_4_.me, bf16[4,16,256]{2,1,0:T(8,128)(2,1)S(1)} %collective-permute-done.13.refs_0_, bf16[4,16,256]{2,1,0:T(8,128)(2,1)S(1)} %collective-permute-done.14.refs_1_, bf16[4,16,256]{2,1,0:T(8,128)(2,1)S(1)} %collective-permute-done.15.refs_2_, ...), custom_call_target="tpu_custom_call" | custom-call | flops 600000000 | bytes 34000000 | tf_op jit(solution)/shard_map/features/pallas_call | solution.py:192
  35.5 1.2 %collective-permute-done.16 = bf16[16,2048]{1,0:T(8,128)(2,1)S(1)} collective-permute-done((bf16[16,2048]{1,0:T(8,128)(2,1)S(1)}, bf16[16,2048]{1,0:T(8,128)(2,1)S(1)}, u32[]{:S(2)}, u32[]{:S(2)}) %collective-permute-start.16) | collective-permute-done | bytes 65568 | tf_op jit(solution)/shard_map/ppermute | solution.py:23
  36.8 1.2 %collective-permute-start.17 = (bf16[16,2048]{1,0:T(8,128)(2,1)S(1)}, bf16[16,2048]{1,0:T(8,128)(2,1)S(1)}, u32[]{:S(2)}, u32[]{:S(2)}) collective-permute-start(bf16[16,2048]{1,0:T(8,128)(2,1)S(1)} %fusion), channel_id=1, source_target_pairs={{0,6},{1,7},{2,4},{3,5},{4,2},{5,3},{6,0},{7,1},{8,14},{9,15},{10,... | collective-permute-start | bytes 196616 | tf_op jit(solution)/shard_map/ppermute | solution.py:23
  38.0 1.0 %collective-permute-start.18 = (bf16[16,2048]{1,0:T(8,128)(2,1)S(1)}, bf16[16,2048]{1,0:T(8,128)(2,1)S(1)}, u32[]{:S(2)}, u32[]{:S(2)}) collective-permute-start(bf16[16,2048]{1,0:T(8,128)(2,1)S(1)} %fusion), channel_id=1, source_target_pairs={{0,4},{1,5},{2,6},{3,7},{4,0},{5,1},{6,2},{7,3},{8,12},{9,13},{10,... | collective-permute-start | bytes 196616 | tf_op jit(solution)/shard_map/ppermute | solution.py:23
  38.9 1.4 %collective-permute-start.19 = (bf16[16,2048]{1,0:T(8,128)(2,1)S(1)}, bf16[16,2048]{1,0:T(8,128)(2,1)S(1)}, u32[]{:S(2)}, u32[]{:S(2)}) collective-permute-start(bf16[16,2048]{1,0:T(8,128)(2,1)S(1)} %fusion), channel_id=1, source_target_pairs={{0,2},{1,3},{2,0},{3,1},{4,6},{5,7},{6,4},{7,5},{8,10},{9,11},{10,... | collective-permute-start | bytes 196616 | tf_op jit(solution)/shard_map/ppermute | solution.py:23
  40.4 2.3 %collective-permute-done.17 = bf16[16,2048]{1,0:T(8,128)(2,1)S(1)} collective-permute-done((bf16[16,2048]{1,0:T(8,128)(2,1)S(1)}, bf16[16,2048]{1,0:T(8,128)(2,1)S(1)}, u32[]{:S(2)}, u32[]{:S(2)}) %collective-permute-start.17) | collective-permute-done | bytes 65568 | tf_op jit(solution)/shard_map/ppermute | solution.py:23
  43.4 2.1 %collective-permute-start.20 = (bf16[16,2048]{1,0:T(8,128)(2,1)S(1)}, bf16[16,2048]{1,0:T(8,128)(2,1)S(1)}, u32[]{:S(2)}, u32[]{:S(2)}) collective-permute-start(bf16[16,2048]{1,0:T(8,128)(2,1)S(1)} %get-tuple-element.35), channel_id=1, source_target_pairs={{0,8},{1,9},{2,10},{3,11},{4,12},{5,13},{6,14},{7,15},{8,0},{9,1},... | collective-permute-start | bytes 196616 | tf_op jit(solution)/shard_map/ppermute | solution.py:23
  45.5 3.8 %collective-permute-done.20.refs_0_ = bf16[16,2048]{1,0:T(8,128)(2,1)S(1)} collective-permute-done((bf16[16,2048]{1,0:T(8,128)(2,1)S(1)}, bf16[16,2048]{1,0:T(8,128)(2,1)S(1)}, u32[]{:S(2)}, u32[]{:S(2)}) %collective-permute-start.20) | collective-permute-done | bytes 65568 | tf_op jit(solution)/shard_map/ppermute | solution.py:23
  49.9 1.2 %collective-permute-done.21 = f32[8,128]{1,0:T(8,128)S(1)} collective-permute-done((f32[8,128]{1,0:T(8,128)S(1)}, f32[8,128]{1,0:T(8,128)S(1)}, u32[]{:S(2)}, u32[]{:S(2)}) %collective-permute-start.21) | collective-permute-done | bytes 4128 | tf_op jit(solution)/shard_map/ppermute | solution.py:23
  (54 shorter events, 6.4 us)
Async XLA Ops:
  0.0 14.9 %copy-start = (bf16[64,512]{1,0:T(8,128)(2,1)S(1)}, bf16[64,512]{1,0:T(8,128)(2,1)}, u32[]{:S(2)}) copy-start(bf16[64,512]{1,0:T(8,128)(2,1)} %refs_3_.5) | copy-start | bytes 196612
  0.0 8.2 %collective-permute-start.1 = (bf16[64,512]{1,0:T(8,128)(2,1)}, bf16[64,512]{1,0:T(8,128)(2,1)S(1)}, u32[]{:S(2)}, u32[]{:S(2)}) collective-permute-start(bf16[64,512]{1,0:T(8,128)(2,1)} %refs_3_.5), channel_id=1, source_target_pairs={{0,12},{1,13},{2,14},{3,15},{4,8},{5,9},{6,10},{7,11},{8,4},{9,5},... | collective-permute-start | bytes 196616 | tf_op jit(solution)/shard_map/ppermute | solution.py:23
  5.1 4.9 %collective-permute-start.3 = (bf16[64,512]{1,0:T(8,128)(2,1)}, bf16[64,512]{1,0:T(8,128)(2,1)S(1)}, u32[]{:S(2)}, u32[]{:S(2)}) collective-permute-start(bf16[64,512]{1,0:T(8,128)(2,1)} %refs_3_.5), channel_id=1, source_target_pairs={{0,4},{1,5},{2,6},{3,7},{4,0},{5,1},{6,2},{7,3},{8,12},{9,13},{10,... | collective-permute-start | bytes 196616 | tf_op jit(solution)/shard_map/ppermute | solution.py:23
  5.1 6.5 %collective-permute-start.5 = (bf16[64,512]{1,0:T(8,128)(2,1)}, bf16[64,512]{1,0:T(8,128)(2,1)S(1)}, u32[]{:S(2)}, u32[]{:S(2)}) collective-permute-start(bf16[64,512]{1,0:T(8,128)(2,1)} %refs_3_.5), channel_id=1, source_target_pairs={{0,8},{1,9},{2,10},{3,11},{4,12},{5,13},{6,14},{7,15},{8,0},{9,1},... | collective-permute-start | bytes 196616 | tf_op jit(solution)/shard_map/ppermute | solution.py:23
  5.7 9.2 %collective-permute-start.7 = (bf16[64,512]{1,0:T(8,128)(2,1)}, bf16[64,512]{1,0:T(8,128)(2,1)S(1)}, u32[]{:S(2)}, u32[]{:S(2)}) collective-permute-start(bf16[64,512]{1,0:T(8,128)(2,1)} %refs_3_.5), channel_id=1, source_target_pairs={{0,2},{1,3},{2,0},{3,1},{4,6},{5,7},{6,4},{7,5},{8,10},{9,11},{10,... | collective-permute-start | bytes 196616 | tf_op jit(solution)/shard_map/ppermute | solution.py:23
  8.2 6.7 %collective-permute-start.2 = (bf16[64,512]{1,0:T(8,128)(2,1)S(1)}, bf16[64,512]{1,0:T(8,128)(2,1)S(1)}, u32[]{:S(2)}, u32[]{:S(2)}) collective-permute-start(bf16[64,512]{1,0:T(8,128)(2,1)S(1)} %collective-permute-done.1.refs_0_), channel_id=1, source_target_pairs={{0,2},{1,3},{2,0},{3,1},{4,6},{5,7},{6,4},{7,5},{8,10},{9,11},{10,... | collective-permute-start | bytes 196616 | tf_op jit(solution)/shard_map/ppermute | solution.py:23
  10.0 5.7 %collective-permute-start.4 = (bf16[64,512]{1,0:T(8,128)(2,1)S(1)}, bf16[64,512]{1,0:T(8,128)(2,1)S(1)}, u32[]{:S(2)}, u32[]{:S(2)}) collective-permute-start(bf16[64,512]{1,0:T(8,128)(2,1)S(1)} %collective-permute-done.3.refs_1_), channel_id=1, source_target_pairs={{0,2},{1,3},{2,0},{3,1},{4,6},{5,7},{6,4},{7,5},{8,10},{9,11},{10,... | collective-permute-start | bytes 196616 | tf_op jit(solution)/shard_map/ppermute | solution.py:23
  11.6 4.3 %collective-permute-start.6 = (bf16[64,512]{1,0:T(8,128)(2,1)S(1)}, bf16[64,512]{1,0:T(8,128)(2,1)S(1)}, u32[]{:S(2)}, u32[]{:S(2)}) collective-permute-start(bf16[64,512]{1,0:T(8,128)(2,1)S(1)} %collective-permute-done.5.refs_2_), channel_id=1, source_target_pairs={{0,2},{1,3},{2,0},{3,1},{4,6},{5,7},{6,4},{7,5},{8,10},{9,11},{10,... | collective-permute-start | bytes 196616 | tf_op jit(solution)/shard_map/ppermute | solution.py:23
  15.6 1.6 %collective-permute-start.9 = (bf16[4,64,512]{2,1,0:T(8,128)(2,1)S(1)}, bf16[4,64,512]{2,1,0:T(8,128)(2,1)S(1)}, u32[]{:S(2)}, u32[]{:S(2)}) collective-permute-start(bf16[4,64,512]{2,1,0:T(8,128)(2,1)S(1)} %join_column.1), channel_id=1, source_target_pairs={{0,1},{1,0},{2,3},{3,2},{4,5},{5,4},{6,7},{7,6},{8,9},{9,8},{10,11... | collective-permute-start | bytes 786440 | tf_op jit(solution)/shard_map/ppermute | solution.py:23
  15.9 1.8 %collective-permute-start.8 = (bf16[4,64,512]{2,1,0:T(8,128)(2,1)S(1)}, bf16[4,64,512]{2,1,0:T(8,128)(2,1)S(1)}, u32[]{:S(2)}, u32[]{:S(2)}) collective-permute-start(bf16[4,64,512]{2,1,0:T(8,128)(2,1)S(1)} %join_across.1), channel_id=1, source_target_pairs={{0,1},{1,0},{2,3},{3,2},{4,5},{5,4},{6,7},{7,6},{8,9},{9,8},{10,11... | collective-permute-start | bytes 786440 | tf_op jit(solution)/shard_map/ppermute | solution.py:23
  16.2 12.5 %collective-permute-start = (f32[8,4096]{1,0:T(8,128)S(1)}, f32[8,4096]{1,0:T(8,128)S(1)}, u32[]{:S(2)}, u32[]{:S(2)}) collective-permute-start(f32[8,4096]{1,0:T(8,128)S(1)} %get-tuple-element.20.targets), channel_id=1, source_target_pairs={{0,1},{1,0},{2,3},{3,2},{4,5},{5,4},{6,7},{7,6},{8,9},{9,8},{10,11... | collective-permute-start | bytes 393224 | tf_op jit(solution)/shard_map/ppermute | solution.py:23
  18.6 12.3 %slice-start = ((s8[33554432]{0:T(1024)(128)(4,1)}), s8[4194304]{0:T(1024)(128)(4,1)S(1)}, s32[]{:S(2)}) async-start(s8[33554432]{0:T(1024)(128)(4,1)} %bitcast.4), calls=%async_computation | async-start | bytes 8388608
  18.7 6.2 %collective-permute-start.10 = (bf16[4,16,256]{2,1,0:T(8,128)(2,1)S(1)}, bf16[4,16,256]{2,1,0:T(8,128)(2,1)S(1)}, u32[]{:S(2)}, u32[]{:S(2)}) collective-permute-start(bf16[4,16,256]{2,1,0:T(8,128)(2,1)S(1)} %hold_rows.1), channel_id=1, source_target_pairs={{0,12},{1,13},{2,14},{3,15},{4,8},{5,9},{6,10},{7,11},{8,4},{9,5},... | collective-permute-start | bytes 98312 | tf_op jit(solution)/shard_map/ppermute | solution.py:23
  21.9 4.8 %collective-permute-start.11 = (bf16[4,16,256]{2,1,0:T(8,128)(2,1)S(1)}, bf16[4,16,256]{2,1,0:T(8,128)(2,1)S(1)}, u32[]{:S(2)}, u32[]{:S(2)}) collective-permute-start(bf16[4,16,256]{2,1,0:T(8,128)(2,1)S(1)} %get-tuple-element.25), channel_id=1, source_target_pairs={{0,8},{1,9},{2,10},{3,11},{4,12},{5,13},{6,14},{7,15},{8,0},{9,1},... | collective-permute-start | bytes 98312 | tf_op jit(solution)/shard_map/ppermute | solution.py:23
  21.9 4.8 %collective-permute-start.12 = (bf16[4,16,256]{2,1,0:T(8,128)(2,1)S(1)}, bf16[4,16,256]{2,1,0:T(8,128)(2,1)S(1)}, u32[]{:S(2)}, u32[]{:S(2)}) collective-permute-start(bf16[4,16,256]{2,1,0:T(8,128)(2,1)S(1)} %get-tuple-element.26), channel_id=1, source_target_pairs={{0,4},{1,5},{2,6},{3,7},{4,0},{5,1},{6,2},{7,3},{8,12},{9,13},{10,... | collective-permute-start | bytes 98312 | tf_op jit(solution)/shard_map/ppermute | solution.py:23
  26.8 3.4 %collective-permute-start.13 = (bf16[4,16,256]{2,1,0:T(8,128)(2,1)S(1)}, bf16[4,16,256]{2,1,0:T(8,128)(2,1)S(1)}, u32[]{:S(2)}, u32[]{:S(2)}) collective-permute-start(bf16[4,16,256]{2,1,0:T(8,128)(2,1)S(1)} %get-tuple-element.28), channel_id=1, source_target_pairs={{0,3},{1,2},{2,1},{3,0},{4,7},{5,6},{6,5},{7,4},{8,11},{9,10},{10,... | collective-permute-start | bytes 98312 | tf_op jit(solution)/shard_map/ppermute | solution.py:23
  26.9 4.1 %collective-permute-start.14 = (bf16[4,16,256]{2,1,0:T(8,128)(2,1)S(1)}, bf16[4,16,256]{2,1,0:T(8,128)(2,1)S(1)}, u32[]{:S(2)}, u32[]{:S(2)}) collective-permute-start(bf16[4,16,256]{2,1,0:T(8,128)(2,1)S(1)} %get-tuple-element.29), channel_id=1, source_target_pairs={{0,2},{1,3},{2,0},{3,1},{4,6},{5,7},{6,4},{7,5},{8,10},{9,11},{10,... | collective-permute-start | bytes 98312 | tf_op jit(solution)/shard_map/ppermute | solution.py:23
  27.6 3.3 %collective-permute-start.15 = (bf16[4,16,256]{2,1,0:T(8,128)(2,1)S(1)}, bf16[4,16,256]{2,1,0:T(8,128)(2,1)S(1)}, u32[]{:S(2)}, u32[]{:S(2)}) collective-permute-start(bf16[4,16,256]{2,1,0:T(8,128)(2,1)S(1)} %get-tuple-element.30), channel_id=1, source_target_pairs={{0,1},{1,0},{2,3},{3,2},{4,5},{5,4},{6,7},{7,6},{8,9},{9,8},{10,11... | collective-permute-start | bytes 98312 | tf_op jit(solution)/shard_map/ppermute | solution.py:23
  35.5 1.3 %collective-permute-start.16 = (bf16[16,2048]{1,0:T(8,128)(2,1)S(1)}, bf16[16,2048]{1,0:T(8,128)(2,1)S(1)}, u32[]{:S(2)}, u32[]{:S(2)}) collective-permute-start(bf16[16,2048]{1,0:T(8,128)(2,1)S(1)} %get-tuple-element.32), channel_id=1, source_target_pairs={{0,1},{1,0},{2,3},{3,2},{4,5},{5,4},{6,7},{7,6},{8,9},{9,8},{10,11... | collective-permute-start | bytes 196616 | tf_op jit(solution)/shard_map/ppermute | solution.py:23
  36.8 5.8 %collective-permute-start.17 = (bf16[16,2048]{1,0:T(8,128)(2,1)S(1)}, bf16[16,2048]{1,0:T(8,128)(2,1)S(1)}, u32[]{:S(2)}, u32[]{:S(2)}) collective-permute-start(bf16[16,2048]{1,0:T(8,128)(2,1)S(1)} %fusion), channel_id=1, source_target_pairs={{0,6},{1,7},{2,4},{3,5},{4,2},{5,3},{6,0},{7,1},{8,14},{9,15},{10,... | collective-permute-start | bytes 196616 | tf_op jit(solution)/shard_map/ppermute | solution.py:23
  38.0 4.7 %collective-permute-start.18 = (bf16[16,2048]{1,0:T(8,128)(2,1)S(1)}, bf16[16,2048]{1,0:T(8,128)(2,1)S(1)}, u32[]{:S(2)}, u32[]{:S(2)}) collective-permute-start(bf16[16,2048]{1,0:T(8,128)(2,1)S(1)} %fusion), channel_id=1, source_target_pairs={{0,4},{1,5},{2,6},{3,7},{4,0},{5,1},{6,2},{7,3},{8,12},{9,13},{10,... | collective-permute-start | bytes 196616 | tf_op jit(solution)/shard_map/ppermute | solution.py:23
  38.9 4.4 %collective-permute-start.19 = (bf16[16,2048]{1,0:T(8,128)(2,1)S(1)}, bf16[16,2048]{1,0:T(8,128)(2,1)S(1)}, u32[]{:S(2)}, u32[]{:S(2)}) collective-permute-start(bf16[16,2048]{1,0:T(8,128)(2,1)S(1)} %fusion), channel_id=1, source_target_pairs={{0,2},{1,3},{2,0},{3,1},{4,6},{5,7},{6,4},{7,5},{8,10},{9,11},{10,... | collective-permute-start | bytes 196616 | tf_op jit(solution)/shard_map/ppermute | solution.py:23
  43.4 5.9 %collective-permute-start.20 = (bf16[16,2048]{1,0:T(8,128)(2,1)S(1)}, bf16[16,2048]{1,0:T(8,128)(2,1)S(1)}, u32[]{:S(2)}, u32[]{:S(2)}) collective-permute-start(bf16[16,2048]{1,0:T(8,128)(2,1)S(1)} %get-tuple-element.35), channel_id=1, source_target_pairs={{0,8},{1,9},{2,10},{3,11},{4,12},{5,13},{6,14},{7,15},{8,0},{9,1},... | collective-permute-start | bytes 196616 | tf_op jit(solution)/shard_map/ppermute | solution.py:23
  49.9 1.2 %collective-permute-start.21 = (f32[8,128]{1,0:T(8,128)S(1)}, f32[8,128]{1,0:T(8,128)S(1)}, u32[]{:S(2)}, u32[]{:S(2)}) collective-permute-start(f32[8,128]{1,0:T(8,128)S(1)} %get-tuple-element.34), channel_id=1, source_target_pairs={{0,1},{1,0},{2,3},{3,2},{4,5},{5,4},{6,7},{7,6},{8,9},{9,8},{10,11... | collective-permute-start | bytes 12296 | tf_op jit(solution)/shard_map/ppermute | solution.py:23
  (7 other events, 86.2 us)
